TPU v7x, 32 devices: a whole 2x2x4 slice. The times are simulated.
32 devices in a mesh: head: 4 (over x, core), ctx: 8 (over z, y).
Axes of the slice: x: 2, y: 2, z: 4, core: 2. Of those that a mesh axis runs over, the one named last changes fastest.
Arguments:
- query_rows: bfloat16 [4096, 4096], P(('head', 'ctx')), may hold values from -6 to 6
- key_rows: bfloat16 [4096, 4096], P(('head', 'ctx')), may hold values from -6 to 6
- value_rows: bfloat16 [4096, 4096], P(('head', 'ctx')), may hold values from -6 to 6
- token_rates: float32 [4096, 16], P(('head', 'ctx')), may hold values from 0.05 to 0.5
- fast_weights: float32 [16, 3, 1024, 256], P('head'), may hold values from -0.4 to 0.4
- momentum: float32 [16, 3, 1024, 256], P('head'), may hold values from -0.12 to 0.12
- out_weight: bfloat16 [4096, 4096], P('head'), may hold values from -0.09375 to 0.09375
Outputs:
- output: bfloat16 [4096, 4096], P(('head', 'ctx'))
All inputs are finite; a program needn't handle non-finite values.
Results may differ from a plain program's by a relative error of at most 0.035.
Values may be sent and summed in bfloat16 or wider, within the bound.
No kernel may reach another device: no remote copies, remote signals or barrier semaphores. Data moves between devices by JAX's collectives and lax.ppermute only.
A program may use at most 128 MiB of HBM per device.

v0:
```python
import jax
import jax.numpy as jnp
from jax import lax
from jax.sharding import PartitionSpec as P


def head_gradient(key_head, value_head, rate_col, weight_bf, rate_scale):
    pre_act = jnp.einsum("td,fd->tf", key_head, weight_bf[0], preferred_element_type=jnp.float32)
    gate_act = jnp.einsum("td,fd->tf", key_head, weight_bf[1], preferred_element_type=jnp.float32)
    sigmoid_pre = jax.nn.sigmoid(pre_act)
    silu_pre = pre_act * sigmoid_pre
    hidden = (silu_pre * gate_act).astype(jnp.bfloat16)
    grad_out = (-(rate_col * rate_scale) * value_head.astype(jnp.float32)).astype(jnp.bfloat16)
    grad_hidden = jnp.einsum(
        "td,fd->tf", grad_out, weight_bf[2], preferred_element_type=jnp.float32
    )
    grad_pre = (
        grad_hidden * gate_act * (sigmoid_pre * (1.0 + pre_act * (1.0 - sigmoid_pre)))
    ).astype(jnp.bfloat16)
    grad_gate = (grad_hidden * silu_pre).astype(jnp.bfloat16)
    return jnp.stack(
        [
            jnp.einsum("tf,td->fd", grad_pre, key_head, preferred_element_type=jnp.float32),
            jnp.einsum("tf,td->fd", grad_gate, key_head, preferred_element_type=jnp.float32),
            jnp.einsum("tf,td->fd", hidden, grad_out, preferred_element_type=jnp.float32),
        ]
    )


def rescale(updated, previous_rows, previous_full, column_new):
    row_old = jnp.sqrt(jnp.sum(jnp.square(previous_rows[:, :2]), axis=3, keepdims=True))
    row_new = jnp.sum(jnp.square(updated[:, :2]), axis=3, keepdims=True)
    first = updated[:, :2] * row_old / jnp.sqrt(row_new + 1e-06)
    column_old = jnp.sqrt(jnp.sum(jnp.square(previous_full[:, 2]), axis=1, keepdims=True))
    second = updated[:, 2] * column_old / jnp.sqrt(column_new + 1e-06)
    return jnp.concatenate([first, second[:, None]], axis=1)


def apply_head(query_head, normed_head):
    pre_act = jnp.einsum(
        "td,fd->tf", query_head, normed_head[0], preferred_element_type=jnp.float32
    )
    gate_act = jnp.einsum(
        "td,fd->tf", query_head, normed_head[1], preferred_element_type=jnp.float32
    )
    hidden = (pre_act * jax.nn.sigmoid(pre_act) * gate_act).astype(jnp.bfloat16)
    return jnp.dot(hidden, normed_head[2], preferred_element_type=jnp.float32).astype(jnp.bfloat16)


def shards(query_rows, key_rows, value_rows, token_rates, fast_weights, momentum, out_weight):
    per_device = fast_weights.shape[0]
    head_width = fast_weights.shape[3]
    group_tokens = key_rows.shape[0] * lax.axis_size("head") * lax.axis_size("ctx")
    rate_scale = float(group_tokens) ** (-0.5)
    query_group, key_group, value_group, rate_group = (
        lax.all_to_all(query_rows, "head", split_axis=1, concat_axis=0, tiled=True),
        lax.all_to_all(key_rows, "head", split_axis=1, concat_axis=0, tiled=True),
        lax.all_to_all(value_rows, "head", split_axis=1, concat_axis=0, tiled=True),
        lax.all_to_all(
            token_rates.astype(jnp.bfloat16), "head", split_axis=1, concat_axis=0, tiled=True
        ).astype(token_rates.dtype),
    )
    gradient_list = []
    for local_head in range(per_device):
        lower = local_head * head_width
        weight_bf = fast_weights[local_head].astype(jnp.bfloat16)
        gradient_list.append(
            head_gradient(
                key_group[:, lower : lower + head_width],
                value_group[:, lower : lower + head_width],
                rate_group[:, local_head : local_head + 1],
                weight_bf,
                rate_scale,
            )
        )
    gradients = jnp.stack(gradient_list)
    summed = lax.psum(gradients.astype(jnp.bfloat16), "ctx").astype(jnp.float32)
    updated = fast_weights - (0.9 * momentum + summed)
    column_new = jnp.sum(jnp.square(updated[:, 2]), axis=1, keepdims=True)
    normed = rescale(updated, fast_weights, fast_weights, column_new).astype(jnp.bfloat16)
    mixed_list = []
    for local_head in range(per_device):
        lower = local_head * head_width
        mixed_list.append(
            apply_head(query_group[:, lower : lower + head_width], normed[local_head])
        )
    mixed = jnp.concatenate(mixed_list, axis=1)
    result = lax.psum_scatter(
        jnp.dot(mixed, out_weight, preferred_element_type=jnp.float32).astype(jnp.bfloat16),
        "head",
        scatter_dimension=0,
        tiled=True,
    )
    return result


def solution(mesh):
    placed = (
        P(("head", "ctx"), None),
        P(("head", "ctx"), None),
        P(("head", "ctx"), None),
        P(("head", "ctx"), None),
        P("head", None, None, None),
        P("head", None, None, None),
        P("head", None),
    )
    return jax.shard_map(
        shards, mesh=mesh, in_specs=placed, out_specs=P(("head", "ctx"), None), check_vma=False
    )
```

profile of v0, /device:TPU:0, one launch (start us, length us, event | category | flops | bytes accessed | tf_op | source)
XLA Modules:
  0.0 386.7 jit_solution(17894647846804697086)
XLA Ops:
  7.8 4.2 %all-to-all-start = ((bf16[128,4,4]{0,2,1:T(4,128)(2,1)}), bf16[128,4,4]{0,2,1:T(4,128)(2,1)S(1)}, u32[]{:S(2)}, u32[]{:S(2)}) async-start(bf16[128,4,4]{0,2,1:T(4,128)(2,1)} %bitcast), calls=%async_computation | async-start | bytes 8192 | tf_op jit(solution)/shard_map/all_to_all | solution.py:59
  12.0 2.3 copy.18
  15.8 3.5 all-to-all-start.2
  19.4 8.1 %convert.70 = bf16[4,3,1024,256]{3,2,1,0:T(8,128)(2,1)} convert(f32[4,3,1024,256]{3,2,1,0:T(8,128)} %param.11) | non-fusion elementwise | flops 3145728 | bytes 18874368 | tf_op jit(solution)/shard_map/convert.39
  28.7 5.1 %all-to-all-done.2 = bf16[128,4,1024]{0,2,1:T(8,128)(2,1)S(1)} async-done(((bf16[128,4,1024]{0,2,1:T(8,128)(2,1)}), bf16[128,4,1024]{0,2,1:T(8,128)(2,1)S(1)}, u32[]{:S(2)}, u32[]{:S(2)}) %all-to-all-start.2) | async-done | bytes 1048608 | tf_op jit(solution)/shard_map/all_to_all | solution.py:57
  33.8 3.5 all-to-all-start.1
  37.9 2.9 fusion.59
  40.8 2.9 fusion.58
  43.7 8.1 %all-to-all-done.1 = bf16[128,4,1024]{0,2,1:T(8,128)(2,1)S(1)} async-done(((bf16[128,4,1024]{0,2,1:T(8,128)(2,1)}), bf16[128,4,1024]{0,2,1:T(8,128)(2,1)S(1)}, u32[]{:S(2)}, u32[]{:S(2)}) %all-to-all-start.1) | async-done | bytes 1048608 | tf_op jit(solution)/shard_map/all_to_all | solution.py:58
  54.2 2.7 fusion.28
  75.0 3.3 pad_maximum_fusion
  80.8 3.5 all-to-all-start.3
  84.4 4.8 %multiply_reduce_fusion.1 = f32[4,2,1024]{2,1,0:T(2,128)S(1)} fusion(f32[4,3,1024,256]{3,2,1,0:T(8,128)} %param.11), kind=kLoop, calls=%fused_computation.3 | loop fusion | flops 4186112 | bytes 8421376 | tf_op jit(solution)/shard_map/reduce_sum | solution.py:31
  89.2 2.5 multiply_reduce_fusion.3
  91.7 7.0 %all-to-all-done.3 = bf16[128,4,1024]{0,2,1:T(8,128)(2,1)S(1)} async-done(((bf16[128,4,1024]{0,2,1:T(8,128)(2,1)}), bf16[128,4,1024]{0,2,1:T(8,128)(2,1)S(1)}, u32[]{:S(2)}, u32[]{:S(2)}) %all-to-all-start.3) | async-done | bytes 1048608 | tf_op jit(solution)/shard_map/all_to_all | solution.py:56
  99.3 191.5 %all-reduce.2.cloned.1.call-done = bf16[4,3,1024,256]{3,2,1,0:T(8,128)(2,1)} async-done(((bf16[4,3,1024,256]{3,2,1,0:T(8,128)(2,1)}), bf16[4,3,1024,256]{3,2,1,0:T(8,128)(2,1)}) %all-reduce.2.cloned.1.call-update) | async-done | bytes 6291472 | tf_op jit(solution)/shard_map/psum | solution.py:77
  290.7 11.0 %add_subtract_fusion = f32[4,3,1024,256]{3,2,1,0:T(8,128)S(1)} fusion(f32[4,3,1024,256]{3,2,1,0:T(8,128)} %param.11, bf16[4,3,1024,256]{3,2,1,0:T(8,128)(2,1)} %all-reduce.2.cloned.1.call-done, f32[4,3,1024,256]{3,2,1,0:T(8,128)} %param.12), kind=kLoop, calls=%fused_computation | loop fusion | flops 12582912 | bytes 44040192 | tf_op jit(solution)/shard_map/sub | solution.py:78
  303.3 2.7 divide_convert_fusion
  315.4 2.8 fusion.36
  318.2 2.8 fusion.37
  321.0 2.8 fusion.38
  323.8 2.8 fusion.39
  326.7 9.5 %convolution_convert_fusion = bf16[512,4096]{1,0:T(8,128)(2,1)} fusion(bf16[1024,4096]{1,0:T(8,128)(2,1)} %param.13, bf16[512,256]{0,1:T(8,128)(2,1)S(1)} %fusion.36, bf16[512,256]{0,1:T(8,128)(2,1)S(1)} %fusion.37, bf16[512,256]{0,1:T(8,128)(2,1)S(1)} %fusion.38, bf16[512,256]{0,1:T(8,128)(2,1)S(1)} %fusion.39), kind=kOutput, calls=%fused_computation.5 | convolution fusion | flops 4301258752 | bytes 13631488 | tf_op jit(solution)/shard_map/dot_general | solution.py:89
  336.2 43.7 %reduce-scatter.2.cloned.1.call-done = bf16[128,4096]{1,0:T(8,128)(2,1)} async-done(((bf16[512,4096]{1,0:T(8,128)(2,1)}), bf16[128,4096]{1,0:T(8,128)(2,1)}) %reduce-scatter.2.cloned.1.call-update) | async-done | bytes 1048592 | tf_op jit(solution)/shard_map/reduce_scatter | solution.py:88
  (62 shorter events, 39.1 us)
Async XLA Ops:
  7.8 8.0 %all-to-all-start = ((bf16[128,4,4]{0,2,1:T(4,128)(2,1)}), bf16[128,4,4]{0,2,1:T(4,128)(2,1)S(1)}, u32[]{:S(2)}, u32[]{:S(2)}) async-start(bf16[128,4,4]{0,2,1:T(4,128)(2,1)} %bitcast), calls=%async_computation | async-start | bytes 8192 | tf_op jit(solution)/shard_map/all_to_all | solution.py:59
  15.8 18.0 %all-to-all-start.2 = ((bf16[128,4,1024]{0,2,1:T(8,128)(2,1)}), bf16[128,4,1024]{0,2,1:T(8,128)(2,1)S(1)}, u32[]{:S(2)}, u32[]{:S(2)}) async-start(bf16[128,4,1024]{0,2,1:T(8,128)(2,1)} %bitcast.8), calls=%async_computation.2 | async-start | bytes 2097152 | tf_op jit(solution)/shard_map/all_to_all | solution.py:57
  19.3 8.1 %copy-start.3 = (bf16[128,4096]{1,0:T(8,128)(2,1)S(1)}, bf16[128,4096]{1,0:T(8,128)(2,1)}, u32[]{:S(2)}) copy-start(bf16[128,4096]{1,0:T(8,128)(2,1)} %param.9) | copy-start | bytes 3145732
  33.8 18.0 %all-to-all-start.1 = ((bf16[128,4,1024]{0,2,1:T(8,128)(2,1)}), bf16[128,4,1024]{0,2,1:T(8,128)(2,1)S(1)}, u32[]{:S(2)}, u32[]{:S(2)}) async-start(bf16[128,4,1024]{0,2,1:T(8,128)(2,1)} %bitcast.4), calls=%async_computation.1 | async-start | bytes 2097152 | tf_op jit(solution)/shard_map/all_to_all | solution.py:58
  37.3 253.4 %all-reduce.2.cloned.1.call-start = ((), (), s32[]{:S(2)}) async-start(), calls=%async_computation.5 | async-start | bytes 12582912 | tf_op jit(solution)/shard_map/psum | solution.py:77
  52.4 1.7 copy-start.1
  54.2 2.7 copy-start.2
  56.9 2.3 slice-start
  57.8 2.2 slice-start.1
  78.3 1.2 copy-start.4
  80.8 18.0 %all-to-all-start.3 = ((bf16[128,4,1024]{0,2,1:T(8,128)(2,1)}), bf16[128,4,1024]{0,2,1:T(8,128)(2,1)S(1)}, u32[]{:S(2)}, u32[]{:S(2)}) async-start(bf16[128,4,1024]{0,2,1:T(8,128)(2,1)} %bitcast.43), calls=%async_computation.3 | async-start | bytes 2097152 | tf_op jit(solution)/shard_map/all_to_all | solution.py:56
  84.3 295.5 %reduce-scatter.2.cloned.1.call-start = ((), (), s32[]{:S(2)}) async-start(), calls=%async_computation.6 | async-start | bytes 5242880 | tf_op jit(solution)/shard_map/reduce_scatter | solution.py:88
  306.0 5.8 %copy-start = (bf16[4,2,1024,256]{3,2,1,0:T(8,128)(2,1)}, bf16[4,2,1024,256]{3,2,1,0:T(8,128)(2,1)S(1)}, u32[]{:S(2)}) copy-start(bf16[4,2,1024,256]{3,2,1,0:T(8,128)(2,1)S(1)} %divide_convert_fusion) | copy-start | bytes 12582916
Sparse Core Ops, SparseCore 0:
  78.4 212.2 all-reduce.1
  336.3 43.4 reduce-scatter.1
where the time goes:
time: 387 us
  waiting for transfers between devices  257 us (66%)
  matrix products  54.9 us (14%)
  other arithmetic  37.6 us (10%)
  starting transfers between devices  14.8 us (4%)
  between operations  13.7 us (4%)
  local copies, waits for them, and re-layouts  8.74 us (2%)
    psum x1, waiting for transfers between devices, shards(): summed = lax.psum(gradients.astype(jnp.bfloat16), 'ctx').astype(jnp.float32)  191 us
    reduce_scatter x1, waiting for transfers between devices, shards(): lax.psum_scatter(jnp.dot(mixed, out_weight, preferred_element_type=jnp.fl...  43.7 us
    another operation x3, other arithmetic  12.5 us
    dot_general x4, matrix products, apply_head(): jnp.dot(hidden, normed_head[2], preferred_element_type=jnp.float32)  11.2 us
    sub x1, other arithmetic, shards(): updated = fast_weights - (0.9 * momentum + summed)  11 us
    dot_general x1, matrix products, shards(): jnp.dot(mixed, out_weight, preferred_element_type=jnp.float32)  9.49 us
    all_to_all x1, waiting for transfers between devices, shards(): lax.all_to_all(value_rows, 'head', split_axis=1, concat_axis=0, tiled=True)  8.06 us
  transfers between devices with their start and end apart: 6, of which 6 were waited for; matrix products, arithmetic and copies ran while one was open for 7% of the time, Pallas kernels for 0%

commit v1 on v0

v1 whole, which is shorter than its diff:
```python
import functools

import jax
import jax.numpy as jnp
from jax import lax
from jax.experimental import pallas as pl
from jax.experimental.pallas import tpu as pltpu
from jax.sharding import Mesh
from jax.sharding import PartitionSpec as P

NT = (((1,), (1,)), ((), ()))


def f32_dot(a, b):
    return jnp.dot(a, b, preferred_element_type=jnp.float32)


def gradient_kernel(blocks, tokens_ref, weight_ref, grad_ref):
    w1 = weight_ref[0].astype(jnp.bfloat16)
    w3 = weight_ref[1].astype(jnp.bfloat16)
    w2 = weight_ref[2].astype(jnp.bfloat16)
    sources, _, rows, width = tokens_ref.shape
    totals = [None] * 3
    for start in range(0, sources, blocks):
        keys = tokens_ref[start : start + blocks, 0].reshape(blocks * rows, width)
        grad_out = tokens_ref[start : start + blocks, 1].reshape(blocks * rows, width)
        pre = lax.dot_general(w1, keys, NT, preferred_element_type=jnp.float32)
        gate = lax.dot_general(w3, keys, NT, preferred_element_type=jnp.float32)
        grad_hidden = lax.dot_general(w2, grad_out, NT, preferred_element_type=jnp.float32)
        sig = jax.nn.sigmoid(pre)
        silu = pre * sig
        hidden = (silu * gate).astype(jnp.bfloat16)
        grad_pre = (grad_hidden * gate * (sig + silu * (1.0 - sig))).astype(jnp.bfloat16)
        grad_gate = (grad_hidden * silu).astype(jnp.bfloat16)
        parts = (f32_dot(grad_pre, keys), f32_dot(grad_gate, keys), f32_dot(hidden, grad_out))
        totals = [p if t is None else t + p for t, p in zip(totals, parts)]
    for m in range(3):
        grad_ref[m] = totals[m].astype(grad_ref.dtype)


def head_gradient(tokens, weight):
    sources, _, rows, width = tokens.shape
    units = weight.shape[1]
    block = min(256, units)
    macs = 6 * sources * rows * width * units
    return pl.pallas_call(
        functools.partial(gradient_kernel, max(1, min(sources, 512 // rows))),
        grid=(units // block,),
        in_specs=[
            pl.BlockSpec(tokens.shape, lambda f: (0, 0, 0, 0)),
            pl.BlockSpec((3, block, width), lambda f: (0, f, 0)),
        ],
        out_specs=pl.BlockSpec((3, block, width), lambda f: (0, f, 0)),
        out_shape=jax.ShapeDtypeStruct(weight.shape, jnp.bfloat16),
        compiler_params=pltpu.CompilerParams(vmem_limit_bytes=24 << 20),
        cost_estimate=pl.CostEstimate(
            flops=2 * macs, bytes_accessed=10 << 20, transcendentals=sources * rows * units
        ),
        name="head_gradient",
    )(tokens, weight)


def apply_kernel(query_ref, normed_ref, out_ref):
    blocks, _, rows, width = query_ref.shape
    query = query_ref[:, 0].reshape(blocks * rows, width)
    pre = lax.dot_general(query, normed_ref[0], NT, preferred_element_type=jnp.float32)
    gate = lax.dot_general(query, normed_ref[1], NT, preferred_element_type=jnp.float32)
    hidden = (pre * jax.nn.sigmoid(pre) * gate).astype(jnp.bfloat16)
    out_ref[...] = f32_dot(hidden, normed_ref[2]).astype(out_ref.dtype).reshape(out_ref.shape)


def apply_head(queries, part, normed):
    sources, _, rows, width = queries.shape
    units = normed.shape[1]
    blocks = max(1, min(sources, 256 // rows))
    macs = 3 * sources * rows * width * units
    return pl.pallas_call(
        apply_kernel,
        grid=(sources // blocks,),
        in_specs=[
            pl.BlockSpec((blocks, 1, rows, width), lambda b: (b, part, 0, 0)),
            pl.BlockSpec(normed.shape, lambda b: (0, 0, 0)),
        ],
        out_specs=pl.BlockSpec((blocks, rows, width), lambda b: (b, 0, 0)),
        out_shape=jax.ShapeDtypeStruct((sources, rows, width), jnp.bfloat16),
        compiler_params=pltpu.CompilerParams(vmem_limit_bytes=24 << 20),
        cost_estimate=pl.CostEstimate(
            flops=2 * macs, bytes_accessed=4 << 20, transcendentals=sources * rows * units
        ),
        name="apply_head",
    )(queries, normed)


def rescale(updated, previous):
    row_old = jnp.sqrt(jnp.sum(jnp.square(previous[:2]), axis=2, keepdims=True))
    row_new = jnp.sum(jnp.square(updated[:2]), axis=2, keepdims=True)
    first = updated[:2] * (row_old / jnp.sqrt(row_new + 1e-06))
    column_old = jnp.sqrt(jnp.sum(jnp.square(previous[2]), axis=0, keepdims=True))
    column_new = jnp.sum(jnp.square(updated[2]), axis=0, keepdims=True)
    second = updated[2] * (column_old / jnp.sqrt(column_new + 1e-06))
    return jnp.concatenate([first, second[None]], axis=0).astype(jnp.bfloat16)


def shards(query_rows, key_rows, value_rows, token_rates, fast_weights, momentum, out_weight):
    sides, heads_here = lax.axis_size("x"), lax.axis_size("hd")
    side, core, head = lax.axis_index("x"), lax.axis_index("core"), lax.axis_index("hd")
    copies = lax.axis_size("rep")
    per_device, _, units, width = fast_weights.shape
    rows = key_rows.shape[0]
    heads = key_rows.shape[1] // width
    rate_scale = float(rows * sides * 2 * heads_here * copies) ** (-0.5)
    swap = [(0, 1), (1, 0)]

    grad_out = (
        -(token_rates * rate_scale)[:, :, None]
        * value_rows.reshape(rows, heads, width).astype(jnp.float32)
    ).astype(jnp.bfloat16)
    payload = jnp.stack(
        [key_rows.reshape(rows, heads, width).transpose(1, 0, 2), grad_out.transpose(1, 0, 2)],
        axis=1,
    )
    tokens = lax.all_to_all(payload, ("x", "hd"), 0, 0, tiled=True)

    owner = head // per_device
    weight_own = lax.dynamic_index_in_dim(fast_weights, head % per_device, 0, keepdims=False)
    momentum_own = lax.dynamic_index_in_dim(momentum, head % per_device, 0, keepdims=False)
    weight = jnp.where(owner == core, weight_own, lax.ppermute(weight_own, "core", swap))
    moment = jnp.where(owner == core, momentum_own, lax.ppermute(momentum_own, "core", swap))
    out_weight_other = lax.ppermute(out_weight, "core", swap)

    strip = heads_here * width
    query_parts = []
    for step in range(sides):
        target = lax.rem(side - step + sides, sides)
        part = lax.dynamic_slice_in_dim(query_rows, target * strip, strip, 1)
        if step:
            part = lax.ppermute(part, "x", [(i, (i - step) % sides) for i in range(sides)])
        query_parts.append(part.reshape(rows, heads_here, width).transpose(1, 0, 2))
    query_ready = jnp.stack(query_parts, axis=1)
    tokens, query_ready = lax.optimization_barrier((tokens, query_ready))
    queries = lax.all_to_all(query_ready, "hd", 0, 0, tiled=True)

    gradient = head_gradient(tokens, weight)
    summed = gradient.astype(jnp.float32) + lax.ppermute(gradient, "core", swap).astype(
        jnp.float32
    )
    if copies > 1:
        summed = lax.psum(summed.astype(jnp.bfloat16), "rep").astype(jnp.float32)
    normed = rescale(weight - (0.9 * moment + summed), weight)

    def project(mixed):
        mine = lax.dynamic_slice_in_dim(mixed, core * per_device, per_device, 0)
        other = lax.dynamic_slice_in_dim(mixed, (1 - core) * per_device, per_device, 0)
        mine = mine.transpose(1, 0, 2).reshape(rows, per_device * width)
        other = other.transpose(1, 0, 2).reshape(rows, per_device * width)
        return f32_dot(mine, out_weight) + f32_dot(other, out_weight_other)

    received = []
    for step in [*range(1, sides), 0]:
        applied = apply_head(queries, step, normed)
        mixed = lax.all_to_all(applied, "hd", 0, 0, tiled=True)
        partial = project(mixed)
        if step:
            partial = lax.ppermute(
                partial.astype(jnp.bfloat16), "x", [(i, (i + step) % sides) for i in range(sides)]
            )
        received.append(partial.astype(jnp.float32))
    return functools.reduce(jnp.add, received).astype(jnp.bfloat16)


def solution(mesh):
    head_axis, ctx_axis = mesh.shape["head"], mesh.shape["ctx"]

    def run(query_rows, key_rows, value_rows, token_rates, fast_weights, momentum, out_weight):
        heads_here = fast_weights.shape[0] // (head_axis // 2)
        fine = Mesh(
            mesh.devices.reshape(head_axis // 2, 2, heads_here, ctx_axis // heads_here),
            ("x", "core", "hd", "rep"),
        )
        token_spec = P(("x", "core", "hd", "rep"), None)
        weight_spec = P(("x", "core"), None, None, None)
        return jax.shard_map(
            shards,
            mesh=fine,
            in_specs=(token_spec,) * 4 + (weight_spec, weight_spec, P(("x", "core"), None)),
            out_specs=token_spec,
            check_vma=False,
        )(query_rows, key_rows, value_rows, token_rates, fast_weights, momentum, out_weight)

    return run
```

time: 387 us -> 190 us (0.49)
  waiting for transfers between devices: 257 us -> 87.5 us
  matrix products: 54.9 us -> 20.7 us
  other arithmetic: 37.6 us -> 11.7 us
  Pallas kernels: 0 us -> 22.1 us
  local copies, waits for them, and re-layouts: 8.74 us -> 23.1 us
  between operations: 13.7 us -> 0.24 us
  starting transfers between devices: 14.8 us -> 23.8 us
    psum x1 -> x0, waiting for transfers between devices: 191 us -> none  [shards(): summed = lax.psum(gradients.astype(jnp.bfloat16), 'ctx').astype(jnp.float32)]
    reduce_scatter x1 -> x0, waiting for transfers between devices: 43.7 us -> none  [shards(): lax.psum_scatter(jnp.dot(mixed, out_weight, preferred_element_type=jnp.fl...]
    all_to_all x4, waiting for transfers between devices: 21.7 us -> 56.5 us  [the longest x2 24.4 us: shards(): mixed = lax.all_to_all(applied, 'hd', 0, 0, tiled=True)]
    dot_general x33 -> x4, matrix products: 54.9 us -> 20.7 us  [f32_dot(): return jnp.dot(a, b, preferred_element_type=jnp.float32)]
    ppermute x0 -> x6, waiting for transfers between devices: none -> 30.9 us  [the longest x1 17.3 us: shards(): lax.ppermute(partial.astype(jnp.bfloat16), 'x', [(i, (i + step) % sides)...]
    pallas_call x0 -> x3, Pallas kernels: none -> 22.1 us  [the longest x1 12.2 us: head_gradient(): pl.pallas_call(functools.partial(gradient_kernel, max(1, min(sources, 512...]
    another operation x6 -> x5, other arithmetic: 16.5 us -> 4.56 us  [the longest x1 2.27 us: shards(): query_ready = jnp.stack(query_parts, axis=1)]
    reduce_sum x4, other arithmetic: 8.73 us -> 1.02 us  [the longest x1 0.35 us: rescale(): row_old = jnp.sqrt(jnp.sum(jnp.square(previous[:2]), axis=2, keepdims=True))]
  transfers between devices with their start and end apart: 6 -> 10, of which waited for: 6 -> 6; matrix products, arithmetic and copies ran while one was open for 7% -> 19% of each run, Pallas kernels for 0% -> 12%
where the time goes in v1:
time: 190 us; the launch traced here: 189 us
  waiting for transfers between devices  87.5 us (46%)
  starting transfers between devices  23.8 us (13%)
  local copies, waits for them, and re-layouts  23.1 us (12%)
  Pallas kernels  22.1 us (12%)
  matrix products  20.7 us (11%)
  other arithmetic  11.7 us (6%)
    all_to_all x2, waiting for transfers between devices, shards(): mixed = lax.all_to_all(applied, 'hd', 0, 0, tiled=True)  24.4 us
    all_to_all x1, waiting for transfers between devices, shards(): queries = lax.all_to_all(query_ready, 'hd', 0, 0, tiled=True)  21.9 us
    dot_general x4, matrix products, f32_dot(): return jnp.dot(a, b, preferred_element_type=jnp.float32)  20.7 us
    ppermute x1, waiting for transfers between devices, shards(): lax.ppermute(partial.astype(jnp.bfloat16), 'x', [(i, (i + step) % sides)...  17.3 us
    ppermute x1, waiting for transfers between devices, shards(): lax.ppermute(part, 'x', [(i, (i - step) % sides) for i in range(sides)])  13.6 us
    pallas_call x1, Pallas kernels, head_gradient(): pl.pallas_call(functools.partial(gradient_kernel, max(1, min(sources, 512...  12.2 us
    all_to_all x1, waiting for transfers between devices, shards(): tokens = lax.all_to_all(payload, ('x', 'hd'), 0, 0, tiled=True)  10.3 us
    pallas_call x2, Pallas kernels, apply_head(): pl.pallas_call(apply_kernel, grid=(sources // blocks,), in_specs=[pl.Bloc...  9.91 us
  transfers between devices with their start and end apart: 10, of which 6 were waited for; matrix products, arithmetic and copies ran while one was open for 19% of the time, Pallas kernels for 12%

profile of v1, /device:TPU:0, one launch (start us, length us, event | category | flops | bytes accessed | tf_op | source)
XLA Modules:
  0.0 189.2 jit_solution(5049578197044803038)
XLA Ops:
  7.9 8.4 %all-to-all-start = ((bf16[16,2,128,256]{3,2,1,0:T(8,128)(2,1)}), bf16[16,2,128,256]{3,2,1,0:T(8,128)(2,1)}, u32[]{:S(2)}, u32[]{:S(2)}) async-start(bf16[16,2,128,256]{3,2,1,0:T(8,128)(2,1)} %pad_maximum_fusion), calls=%async_computation | async-start | bytes 4194304 | tf_op jit(solution)/shard_map/all_to_all | solution.py:122
  16.3 2.1 %dynamic-slice_bitcast_fusion.1 = f32[3,1024,256]{2,1,0:T(8,128)S(1)} fusion(f32[4,3,1024,256]{3,2,1,0:T(8,128)} %param.11, s32[]{:T(128)S(6)} %select_n.49), kind=kLoop, calls=%fused_computation.5 | loop fusion | bytes 6291460 | tf_op jit(solution)/shard_map/jit(dynamic_index_in_dim)/squeeze | solution.py:125
  18.9 2.3 %constant_dynamic-slice_fusion.1 = (bf16[128,2048]{1,0:T(8,128)(2,1)}, bf16[128,2048]{1,0:T(8,128)(2,1)}) fusion(bf16[128,4096]{1,0:T(8,128)(2,1)} %param.7, s32[]{:T(128)S(6)} %select_n.44, s32[]{:T(128)S(6)} %select_n.45), kind=kLoop, calls=%fused_computation.28 | loop fusion | bytes 2097160 | tf_op jit(solution)/shard_map/dynamic_slice | solution.py:135
  25.1 3.8 %dynamic-slice_bitcast_fusion = f32[3,1024,256]{2,1,0:T(8,128)} fusion(f32[4,3,1024,256]{3,2,1,0:T(8,128)} %param.12, s32[]{:T(128)S(6)} %select_n.49), kind=kLoop, calls=%fused_computation.4 | loop fusion | bytes 6291460 | tf_op jit(solution)/shard_map/jit(dynamic_index_in_dim)/squeeze | solution.py:126
  31.0 2.1 %copy.13 = bf16[128,8,256]{2,0,1:T(8,128)(2,1)} copy(bf16[128,8,256]{0,2,1:T(8,128)(2,1)} %bitcast.49) | data formatting | bytes 1048576 | tf_op jit(solution)/shard_map/reshape | solution.py:138
  33.1 13.6 %collective-permute-done = bf16[128,2048]{0,1:T(8,128)(2,1)} collective-permute-done((bf16[128,2048]{0,1:T(8,128)(2,1)}, bf16[128,2048]{0,1:T(8,128)(2,1)}, u32[]{:S(2)}, u32[]{:S(2)}) %collective-permute-start) | collective-permute-done | bytes 524320 | tf_op jit(solution)/shard_map/ppermute | solution.py:137
  48.7 2.3 %pad_maximum_fusion.2 = bf16[8,2,128,256]{3,2,1,0:T(8,128)(2,1)} fusion(bf16[8,1,128,256]{3,2,1,0:T(8,128)(2,1)} %bitcast.51, bf16[8,1,128,256]{3,2,1,0:T(8,128)(2,1)} %bitcast.50), kind=kLoop, calls=%fused_computation.18 | loop fusion | flops 524288 | bytes 2097152 | tf_op jit(solution)/shard_map/stack | solution.py:139
  51.0 2.3 %broadcast_select_fusion.weight_ref = f32[3,1024,256]{2,1,0:T(8,128)S(1)} fusion(f32[3,1024,256]{2,1,0:T(8,128)} %collective-permute-done.1, pred[]{:T(512)S(6)} %eq.7, f32[4,3,1024,256]{3,2,1,0:T(8,128)} %param.11, s32[]{:T(128)S(6)} %select_n.49), kind=kLoop, calls=%fused_computation.14 | loop fusion | flops 786432 | bytes 9437189 | tf_op jit(solution)/shard_map/jit(_where)/select_n | solution.py:127
  53.3 10.3 %all-to-all-done.tokens_ref = bf16[16,2,128,256]{3,2,1,0:T(8,128)(2,1)} async-done(((bf16[16,2,128,256]{3,2,1,0:T(8,128)(2,1)}), bf16[16,2,128,256]{3,2,1,0:T(8,128)(2,1)}, u32[]{:S(2)}, u32[]{:S(2)}) %all-to-all-start) | async-done | bytes 2097184 | tf_op jit(solution)/shard_map/all_to_all | solution.py:122
  63.5 12.2 %head_gradient.1 = bf16[3,1024,256]{2,1,0:T(8,128)(2,1)} custom-call(bf16[16,2,128,256]{3,2,1,0:T(8,128)(2,1)} %all-to-all-done.tokens_ref, f32[3,1024,256]{2,1,0:T(8,128)S(1)} %broadcast_select_fusion.weight_ref), custom_call_target="tpu_custom_call" | custom-call | flops 6442450944 | bytes 10485760 | tf_op jit(solution)/shard_map/head_gradient/pallas_call | solution.py:46
  76.2 4.3 %all-to-all-start.1 = ((bf16[8,2,128,256]{3,2,1,0:T(8,128)(2,1)}), bf16[8,2,128,256]{3,2,1,0:T(8,128)(2,1)}, u32[]{:S(2)}, u32[]{:S(2)}) async-start(bf16[8,2,128,256]{3,2,1,0:T(8,128)(2,1)} %pad_maximum_fusion.2), calls=%async_computation.1 | async-start | bytes 2097152 | tf_op jit(solution)/shard_map/all_to_all | solution.py:141
  80.5 3.7 %add_subtract_fusion = f32[3,1024,256]{2,1,0:T(8,128)S(1)} fusion(f32[3,1024,256]{2,1,0:T(8,128)S(1)} %broadcast_select_fusion.weight_ref, bf16[3,1024,256]{2,1,0:T(8,128)(2,1)} %collective-permute-done.3, bf16[3,1024,256]{2,1,0:T(8,128)(2,1)} %head_gradient.1, f32[3,1024,256]{2,1,0:T(8,128)} %collective-permute-done.2, pred[]{:T(512)S(6)} %eq.7, ...), kind=kLoop, calls=%fused_computation.3 | loop fusion | flops 5505024 | bytes 15728645 | tf_op jit(solution)/shard_map/sub | solution.py:149
  85.4 21.9 %all-to-all-done.1.query_ref = bf16[8,2,128,256]{3,2,1,0:T(8,128)(2,1)} async-done(((bf16[8,2,128,256]{3,2,1,0:T(8,128)(2,1)}), bf16[8,2,128,256]{3,2,1,0:T(8,128)(2,1)}, u32[]{:S(2)}, u32[]{:S(2)}) %all-to-all-start.1) | async-done | bytes 1048608 | tf_op jit(solution)/shard_map/all_to_all | solution.py:141
  107.2 4.9 %apply_head.3 = bf16[8,128,256]{2,1,0:T(8,128)(2,1)} custom-call(bf16[8,2,128,256]{3,2,1,0:T(8,128)(2,1)} %all-to-all-done.1.query_ref, bf16[3,1024,256]{2,1,0:T(8,128)(2,1)S(1)} %pad_maximum_fusion.1.normed_ref), custom_call_target="tpu_custom_call" | custom-call | flops 1610612736 | bytes 4194304 | tf_op jit(solution)/shard_map/apply_head/pallas_call | solution.py:77
  112.2 3.6 %all-to-all-start.3 = ((bf16[8,128,256]{2,1,0:T(8,128)(2,1)}), bf16[8,128,256]{2,1,0:T(8,128)(2,1)S(1)}, u32[]{:S(2)}, u32[]{:S(2)}) async-start(bf16[8,128,256]{2,1,0:T(8,128)(2,1)} %apply_head.3), calls=%async_computation.3 | async-start | bytes 1048576 | tf_op jit(solution)/shard_map/all_to_all | solution.py:161
  115.8 5.0 %apply_head.2 = bf16[8,128,256]{2,1,0:T(8,128)(2,1)} custom-call(bf16[8,2,128,256]{3,2,1,0:T(8,128)(2,1)} %all-to-all-done.1.query_ref, bf16[3,1024,256]{2,1,0:T(8,128)(2,1)S(1)} %pad_maximum_fusion.1.normed_ref), custom_call_target="tpu_custom_call" | custom-call | flops 1610612736 | bytes 4194304 | tf_op jit(solution)/shard_map/apply_head/pallas_call | solution.py:77
  120.8 9.8 %all-to-all-done.3 = bf16[8,128,256]{2,1,0:T(8,128)(2,1)S(1)} async-done(((bf16[8,128,256]{2,1,0:T(8,128)(2,1)}), bf16[8,128,256]{2,1,0:T(8,128)(2,1)S(1)}, u32[]{:S(2)}, u32[]{:S(2)}) %all-to-all-start.3) | async-done | bytes 524320 | tf_op jit(solution)/shard_map/all_to_all | solution.py:161
  130.5 3.7 %all-to-all-start.2 = ((bf16[8,128,256]{2,1,0:T(8,128)(2,1)}), bf16[8,128,256]{2,1,0:T(8,128)(2,1)S(1)}, u32[]{:S(2)}, u32[]{:S(2)}) async-start(bf16[8,128,256]{2,1,0:T(8,128)(2,1)} %apply_head.2), calls=%async_computation.2 | async-start | bytes 1048576 | tf_op jit(solution)/shard_map/all_to_all | solution.py:161
  134.2 14.6 %all-to-all-done.2 = bf16[8,128,256]{2,1,0:T(8,128)(2,1)S(1)} async-done(((bf16[8,128,256]{2,1,0:T(8,128)(2,1)}), bf16[8,128,256]{2,1,0:T(8,128)(2,1)S(1)}, u32[]{:S(2)}, u32[]{:S(2)}) %all-to-all-start.2) | async-done | bytes 524320 | tf_op jit(solution)/shard_map/all_to_all | solution.py:161
  149.3 4.7 %fusion.4 = f32[128,4096]{1,0:T(8,128)S(1)} fusion(bf16[128,1024]{0,1:T(8,128)(2,1)S(1)} %bitcast.54, bf16[1024,4096]{1,0:T(8,128)(2,1)} %param.13), kind=kOutput, calls=%fused_computation.30 | convolution fusion | flops 1073741824 | bytes 10747904 | tf_op jit(solution)/shard_map/dot_general | solution.py:15
  154.0 5.6 %fusion = bf16[128,4096]{1,0:T(8,128)(2,1)} fusion(f32[128,4096]{1,0:T(8,128)S(1)} %fusion.4, bf16[128,1024]{0,1:T(8,128)(2,1)S(1)} %bitcast.52, bf16[1024,4096]{1,0:T(8,128)(2,1)} %collective-permute-done.4), kind=kOutput, calls=%fused_computation.2 | convolution fusion | flops 1074790400 | bytes 11796480 | tf_op jit(solution)/shard_map/dot_general | solution.py:15
  161.5 4.7 %fusion.5 = f32[128,4096]{1,0:T(8,128)S(1)} fusion(bf16[128,1024]{0,1:T(8,128)(2,1)S(1)} %bitcast.53, bf16[1024,4096]{1,0:T(8,128)(2,1)} %param.13), kind=kOutput, calls=%fused_computation.31 | convolution fusion | flops 1073741824 | bytes 10747904 | tf_op jit(solution)/shard_map/dot_general | solution.py:15
  166.1 17.3 %collective-permute-done.5 = bf16[128,4096]{1,0:T(8,128)(2,1)S(1)} collective-permute-done((bf16[128,4096]{1,0:T(8,128)(2,1)}, bf16[128,4096]{1,0:T(8,128)(2,1)S(1)}, u32[]{:S(2)}, u32[]{:S(2)}) %collective-permute-start.5) | collective-permute-done | bytes 1048608 | tf_op jit(solution)/shard_map/ppermute | solution.py:164
  183.4 5.7 %add_convert_fusion = bf16[128,4096]{1,0:T(8,128)(2,1)} fusion(bf16[128,4096]{1,0:T(8,128)(2,1)S(1)} %collective-permute-done.5, f32[128,4096]{1,0:T(8,128)S(1)} %fusion.5, bf16[128,1024]{0,1:T(8,128)(2,1)S(1)} %bitcast.55, bf16[1024,4096]{1,0:T(8,128)(2,1)} %collective-permute-done.4), kind=kOutput, calls=%fused_computation.9 | convolution fusion | flops 1075838976 | bytes 12845056 | tf_op jit(solution)/shard_map/dot_general | solution.py:15
  (38 shorter events, 20.3 us)
Async XLA Ops:
  0.0 2.2 %copy-start.1 = (f32[128,16]{0,1:T(8,128)S(1)}, f32[128,16]{0,1:T(8,128)}, u32[]{:S(2)}) copy-start(f32[128,16]{0,1:T(8,128)} %param.10) | copy-start | bytes 24580
  5.1 1.2 copy-start
  7.9 55.7 %all-to-all-start = ((bf16[16,2,128,256]{3,2,1,0:T(8,128)(2,1)}), bf16[16,2,128,256]{3,2,1,0:T(8,128)(2,1)}, u32[]{:S(2)}, u32[]{:S(2)}) async-start(bf16[16,2,128,256]{3,2,1,0:T(8,128)(2,1)} %pad_maximum_fusion), calls=%async_computation | async-start | bytes 4194304 | tf_op jit(solution)/shard_map/all_to_all | solution.py:122
  18.4 32.6 %collective-permute-start.1 = (f32[3,1024,256]{2,1,0:T(8,128)S(1)}, f32[3,1024,256]{2,1,0:T(8,128)}, u32[]{:S(2)}, u32[]{:S(2)}) collective-permute-start(f32[3,1024,256]{2,1,0:T(8,128)S(1)} %dynamic-slice_bitcast_fusion.1), channel_id=1, source_target_pairs={{0,8},{8,0},{1,9},{9,1},{2,10},{10,2},{3,11},{11,3},{4,12},{12,4},... | collective-permute-start | bytes 9437192 | tf_op jit(solution)/shard_map/ppermute | solution.py:127
  18.4 135.5 %collective-permute-start.4 = (bf16[1024,4096]{1,0:T(8,128)(2,1)}, bf16[1024,4096]{1,0:T(8,128)(2,1)}, u32[]{:S(2)}, u32[]{:S(2)}) collective-permute-start(bf16[1024,4096]{1,0:T(8,128)(2,1)} %param.13), channel_id=1, source_target_pairs={{0,8},{8,0},{1,9},{9,1},{2,10},{10,2},{3,11},{11,3},{4,12},{12,4},... | collective-permute-start | bytes 25165832 | tf_op jit(solution)/shard_map/ppermute | solution.py:129
  23.3 23.4 %collective-permute-start = (bf16[128,2048]{0,1:T(8,128)(2,1)}, bf16[128,2048]{0,1:T(8,128)(2,1)}, u32[]{:S(2)}, u32[]{:S(2)}) collective-permute-start(bf16[128,2048]{0,1:T(8,128)(2,1)} %copy.21), channel_id=1, source_target_pairs={{0,16},{16,0},{1,17},{17,1},{2,18},{18,2},{3,19},{19,3},{4,20},{20... | collective-permute-start | bytes 1572872 | tf_op jit(solution)/shard_map/ppermute | solution.py:137
  28.9 51.6 %collective-permute-start.2 = (f32[3,1024,256]{2,1,0:T(8,128)}, f32[3,1024,256]{2,1,0:T(8,128)}, u32[]{:S(2)}, u32[]{:S(2)}) collective-permute-start(f32[3,1024,256]{2,1,0:T(8,128)} %dynamic-slice_bitcast_fusion), channel_id=1, source_target_pairs={{0,8},{8,0},{1,9},{9,1},{2,10},{10,2},{3,11},{11,3},{4,12},{12,4},... | collective-permute-start | bytes 9437192 | tf_op jit(solution)/shard_map/ppermute | solution.py:128
  75.7 4.8 %collective-permute-start.3 = (bf16[3,1024,256]{2,1,0:T(8,128)(2,1)}, bf16[3,1024,256]{2,1,0:T(8,128)(2,1)}, u32[]{:S(2)}, u32[]{:S(2)}) collective-permute-start(bf16[3,1024,256]{2,1,0:T(8,128)(2,1)} %head_gradient.1), channel_id=1, source_target_pairs={{0,8},{8,0},{1,9},{9,1},{2,10},{10,2},{3,11},{11,3},{4,12},{12,4},... | collective-permute-start | bytes 4718600 | tf_op jit(solution)/shard_map/ppermute | solution.py:144
  76.2 31.0 %all-to-all-start.1 = ((bf16[8,2,128,256]{3,2,1,0:T(8,128)(2,1)}), bf16[8,2,128,256]{3,2,1,0:T(8,128)(2,1)}, u32[]{:S(2)}, u32[]{:S(2)}) async-start(bf16[8,2,128,256]{3,2,1,0:T(8,128)(2,1)} %pad_maximum_fusion.2), calls=%async_computation.1 | async-start | bytes 2097152 | tf_op jit(solution)/shard_map/all_to_all | solution.py:141
  112.2 18.4 %all-to-all-start.3 = ((bf16[8,128,256]{2,1,0:T(8,128)(2,1)}), bf16[8,128,256]{2,1,0:T(8,128)(2,1)S(1)}, u32[]{:S(2)}, u32[]{:S(2)}) async-start(bf16[8,128,256]{2,1,0:T(8,128)(2,1)} %apply_head.3), calls=%async_computation.3 | async-start | bytes 1048576 | tf_op jit(solution)/shard_map/all_to_all | solution.py:161
  130.5 18.3 %all-to-all-start.2 = ((bf16[8,128,256]{2,1,0:T(8,128)(2,1)}), bf16[8,128,256]{2,1,0:T(8,128)(2,1)S(1)}, u32[]{:S(2)}, u32[]{:S(2)}) async-start(bf16[8,128,256]{2,1,0:T(8,128)(2,1)} %apply_head.2), calls=%async_computation.2 | async-start | bytes 1048576 | tf_op jit(solution)/shard_map/all_to_all | solution.py:161
  159.6 23.8 %collective-permute-start.5 = (bf16[128,4096]{1,0:T(8,128)(2,1)}, bf16[128,4096]{1,0:T(8,128)(2,1)S(1)}, u32[]{:S(2)}, u32[]{:S(2)}) collective-permute-start(bf16[128,4096]{1,0:T(8,128)(2,1)} %fusion), channel_id=1, source_target_pairs={{0,16},{16,0},{1,17},{17,1},{2,18},{18,2},{3,19},{19,3},{4,20},{20... | collective-permute-start | bytes 3145736 | tf_op jit(solution)/shard_map/ppermute | solution.py:164

commit v2 on v1

v2 whole, which is shorter than its diff:
```python
import functools

import jax
import jax.numpy as jnp
from jax import lax
from jax.experimental import pallas as pl
from jax.experimental.pallas import tpu as pltpu
from jax.sharding import Mesh
from jax.sharding import PartitionSpec as P

NT = (((1,), (1,)), ((), ()))
VMEM = 14 << 20
SMALL = pl.CostEstimate(flops=1024, bytes_accessed=1024, transcendentals=0)


def f32_dot(a, b):
    return jnp.dot(a, b, preferred_element_type=jnp.float32)


def sigmoid(x):
    return 0.5 * jnp.tanh(0.5 * x) + 0.5


def pack_kernel(scale, group, key_ref, value_ref, rate_ref, out_ref):
    rates = rate_ref[...].T
    width = out_ref.shape[3]
    columns = lax.broadcasted_iota(jnp.int32, rates.shape, 1)
    for i in range(group):
        head = pl.program_id(0) * group + i
        rate = jnp.sum(jnp.where(columns == head, rates, 0.0), axis=1, keepdims=True)
        piece = slice(i * width, (i + 1) * width)
        out_ref[i, 0] = key_ref[:, piece]
        out_ref[i, 1] = (-(rate * scale) * value_ref[:, piece].astype(jnp.float32)).astype(
            out_ref.dtype
        )


def pack(key_rows, value_rows, token_rates, width, scale):
    rows, columns = key_rows.shape
    heads = columns // width
    group = 4 if heads % 4 == 0 else 1
    return pl.pallas_call(
        functools.partial(pack_kernel, scale, group),
        grid=(heads // group,),
        in_specs=[
            pl.BlockSpec((rows, group * width), lambda h: (0, h)),
            pl.BlockSpec((rows, group * width), lambda h: (0, h)),
            pl.BlockSpec(token_rates.shape[::-1], lambda h: (0, 0)),
        ],
        out_specs=pl.BlockSpec((group, 2, rows, width), lambda h: (h, 0, 0, 0)),
        out_shape=jax.ShapeDtypeStruct((heads, 2, rows, width), key_rows.dtype),
        compiler_params=pltpu.CompilerParams(vmem_limit_bytes=VMEM),
        name="pack",
    )(*(pltpu.with_memory_space_constraint(a, pltpu.HBM) for a in (key_rows, value_rows)), token_rates.T)


def turn_kernel(side_ref, rows_ref, out_ref):
    width = out_ref.shape[3]
    for i in range(out_ref.shape[1]):
        out_ref[0, i] = rows_ref[:, i * width : (i + 1) * width]


def turn(query_rows, side, sides, width):
    rows, columns = query_rows.shape
    strip = columns // sides
    return pl.pallas_call(
        turn_kernel,
        grid_spec=pltpu.PrefetchScalarGridSpec(
            num_scalar_prefetch=1,
            grid=(sides,),
            in_specs=[
                pl.BlockSpec((rows, strip), lambda d, s: (0, lax.rem(s[0] - d + sides, sides)))
            ],
            out_specs=pl.BlockSpec((1, strip // width, rows, width), lambda d, s: (d, 0, 0, 0)),
        ),
        out_shape=jax.ShapeDtypeStruct((sides, strip // width, rows, width), query_rows.dtype),
        compiler_params=pltpu.CompilerParams(vmem_limit_bytes=VMEM),
        cost_estimate=SMALL,
        name="turn",
    )(side[None], pltpu.with_memory_space_constraint(query_rows, pltpu.HBM))


def hold_kernel(own_ref, other_ref, after_ref, out_ref, sems):
    core = lax.axis_index("core")
    depth = own_ref.shape[0]
    first = pltpu.make_async_copy(own_ref, out_ref.at[pl.ds(core * depth, depth)], sems.at[0])
    second = pltpu.make_async_copy(
        other_ref, out_ref.at[pl.ds((1 - core) * depth, depth)], sems.at[1]
    )
    first.start()
    second.start()
    first.wait()
    second.wait()


def hold(own, other, after):
    depth, columns = own.shape
    own = pltpu.with_memory_space_constraint(own, pltpu.HBM)
    other = pltpu.with_memory_space_constraint(other, pltpu.HBM)
    return pl.pallas_call(
        hold_kernel,
        in_specs=[pl.BlockSpec(memory_space=pltpu.HBM)] * 2 + [pl.BlockSpec(memory_space=pl.ANY)],
        out_specs=pl.BlockSpec(memory_space=pltpu.VMEM),
        out_shape=pltpu.VMEM((2 * depth, columns), own.dtype),
        scratch_shapes=[pltpu.SemaphoreType.DMA((2,))],
        compiler_params=pltpu.CompilerParams(vmem_limit_bytes=VMEM),
        cost_estimate=SMALL,
        name="hold",
    )(own, other, after)


def gradient_kernel(blocks, tokens_ref, weight_ref, grad_ref):
    w1, w3, w2 = (weight_ref[m].astype(jnp.bfloat16) for m in range(3))
    sources, _, rows, width = tokens_ref.shape
    totals = [None] * 3
    for start in range(0, sources, blocks):
        keys = tokens_ref[start : start + blocks, 0].reshape(blocks * rows, width)
        grad_out = tokens_ref[start : start + blocks, 1].reshape(blocks * rows, width)
        pre = lax.dot_general(w1, keys, NT, preferred_element_type=jnp.float32)
        gate = lax.dot_general(w3, keys, NT, preferred_element_type=jnp.float32)
        grad_hidden = lax.dot_general(w2, grad_out, NT, preferred_element_type=jnp.float32)
        sig = sigmoid(pre)
        silu = pre * sig
        hidden = (silu * gate).astype(jnp.bfloat16)
        grad_pre = (grad_hidden * gate * (sig + silu * (1.0 - sig))).astype(jnp.bfloat16)
        grad_gate = (grad_hidden * silu).astype(jnp.bfloat16)
        parts = (f32_dot(grad_pre, keys), f32_dot(grad_gate, keys), f32_dot(hidden, grad_out))
        totals = [p if t is None else t + p for t, p in zip(totals, parts)]
    for m in range(3):
        grad_ref[m] = totals[m].astype(grad_ref.dtype)


def head_gradient(tokens, weight):
    sources, _, rows, width = tokens.shape
    units = weight.shape[1]
    block = min(256, units)
    return pl.pallas_call(
        functools.partial(gradient_kernel, max(1, min(sources, 512 // rows))),
        grid=(units // block,),
        in_specs=[
            pl.BlockSpec(tokens.shape, lambda f: (0, 0, 0, 0)),
            pl.BlockSpec((3, block, width), lambda f: (0, f, 0)),
        ],
        out_specs=pl.BlockSpec((3, block, width), lambda f: (0, f, 0)),
        out_shape=jax.ShapeDtypeStruct(weight.shape, jnp.bfloat16),
        compiler_params=pltpu.CompilerParams(vmem_limit_bytes=VMEM),
        cost_estimate=SMALL,
        name="head_gradient",
    )(*(pltpu.with_memory_space_constraint(a, pltpu.HBM) for a in (tokens, weight)))


def update_kernel(terms, weight_ref, momentum_ref, *refs):
    out_ref = refs[-1]
    previous = weight_ref[0]
    change = 0.9 * momentum_ref[0]
    for ref in refs[:terms]:
        change = change + ref[0].astype(jnp.float32)
    updated = previous - change

    def scaled(axis):
        old = jnp.sum(jnp.square(previous), axis=axis, keepdims=True)
        new = jnp.sum(jnp.square(updated), axis=axis, keepdims=True)
        out_ref[0] = (updated * (jnp.sqrt(old) / jnp.sqrt(new + 1e-06))).astype(out_ref.dtype)

    @pl.when(pl.program_id(0) < 2)
    def _():
        scaled(1)

    @pl.when(pl.program_id(0) == 2)
    def _():
        scaled(0)


def update(weight, moment, gradients, after):
    _, units, width = weight.shape
    spec = pl.BlockSpec((1, units, width), lambda m: (m, 0, 0))
    return pl.pallas_call(
        functools.partial(update_kernel, len(gradients)),
        grid=(3,),
        in_specs=[spec] * (2 + len(gradients)) + [pl.BlockSpec(memory_space=pl.ANY)] * len(after),
        out_specs=spec,
        out_shape=jax.ShapeDtypeStruct(weight.shape, jnp.bfloat16),
        compiler_params=pltpu.CompilerParams(vmem_limit_bytes=VMEM),
        cost_estimate=SMALL,
        name="update",
    )(weight, moment, *gradients, *after)


def apply_kernel(part, offsets, normed_ref, query_ref, *refs):
    out_refs = refs[-len(offsets) :]
    head = lax.axis_index("hd")
    _, _, rows, _ = query_ref.shape
    group = max(1, min(len(offsets), 512 // rows))
    for start in range(0, len(offsets), group):
        picked = offsets[start : start + group]
        query = jnp.concatenate([query_ref[jnp.bitwise_xor(head, i), part] for i in picked], axis=0)
        pre = lax.dot_general(query, normed_ref[0], NT, preferred_element_type=jnp.float32)
        gate = lax.dot_general(query, normed_ref[1], NT, preferred_element_type=jnp.float32)
        hidden = (pre * sigmoid(pre) * gate).astype(jnp.bfloat16)
        out = f32_dot(hidden, normed_ref[2]).astype(jnp.bfloat16)
        for n in range(len(picked)):
            out_refs[start + n][...] = out[n * rows : (n + 1) * rows]


def apply_head(queries, part, offsets, normed, after):
    _, _, rows, width = queries.shape
    whole = pl.BlockSpec(memory_space=pltpu.VMEM)
    return pl.pallas_call(
        functools.partial(apply_kernel, part, offsets),
        in_specs=[whole, whole] + [pl.BlockSpec(memory_space=pl.ANY)] * len(after),
        out_specs=[whole] * len(offsets),
        out_shape=[jax.ShapeDtypeStruct((rows, width), jnp.bfloat16)] * len(offsets),
        compiler_params=pltpu.CompilerParams(vmem_limit_bytes=VMEM),
        cost_estimate=SMALL,
        name="apply_head",
    )(normed, queries, *after)


def project_kernel(block, start, terms, weight_ref, *refs):
    mixed_refs, out_ref, depth_ref = refs[:terms], refs[-2], refs[-1]
    head = lax.axis_index("hd")
    rows, width = mixed_refs[0].shape
    for i, ref in enumerate(mixed_refs):
        depth_ref[jnp.bitwise_xor(head, i)] = ref[...]
    mixed = jnp.concatenate([depth_ref[i] for i in range(len(mixed_refs))], axis=1)
    for first in range(0, out_ref.shape[1], block):
        part = f32_dot(mixed, weight_ref[:, start + first : start + first + block])
        out_ref[:, first : first + block] = part.astype(out_ref.dtype)


def project(mixed, weight, start, stop, dtype, after):
    rows, width = mixed[0].shape
    block = min(512, stop - start)
    whole = pl.BlockSpec(memory_space=pltpu.VMEM)
    weight = pltpu.with_memory_space_constraint(weight, pltpu.VMEM)
    return pl.pallas_call(
        functools.partial(project_kernel, block, start, len(mixed)),
        in_specs=[whole] * (1 + len(mixed)) + [pl.BlockSpec(memory_space=pl.ANY)] * len(after),
        out_specs=whole,
        out_shape=jax.ShapeDtypeStruct((rows, stop - start), dtype),
        scratch_shapes=[pltpu.VMEM((len(mixed), rows, width), mixed[0].dtype)],
        compiler_params=pltpu.CompilerParams(vmem_limit_bytes=VMEM),
        cost_estimate=SMALL,
        name="project",
    )(weight, *mixed, *after)


def shards(query_rows, key_rows, value_rows, token_rates, fast_weights, momentum, out_weight):
    sides, heads_here = lax.axis_size("x"), lax.axis_size("hd")
    side, core, head = lax.axis_index("x"), lax.axis_index("core"), lax.axis_index("hd")
    copies = lax.axis_size("rep")
    per_device, _, units, width = fast_weights.shape
    rows = key_rows.shape[0]
    rate_scale = float(rows * sides * 2 * heads_here * copies) ** (-0.5)
    swap = [(0, 1), (1, 0)]

    payload = pack(key_rows, value_rows, token_rates, width, rate_scale)
    tokens = lax.all_to_all(payload, ("x", "hd"), 0, 0, tiled=True)

    owned = head // per_device == core
    weight = lax.dynamic_index_in_dim(fast_weights, head % per_device, 0, keepdims=False)
    moment = lax.dynamic_index_in_dim(momentum, head % per_device, 0, keepdims=False)
    weight = jnp.where(owned, weight, lax.ppermute(weight, "core", swap))
    moment = jnp.where(owned, moment, lax.ppermute(moment, "core", swap))
    out_weight_other = lax.ppermute(out_weight, "core", swap)

    turned = turn(query_rows, side, sides, width)
    query_parts = [turned[0]] + [
        lax.ppermute(turned[d], "x", [(i, (i - d) % sides) for i in range(sides)])
        for d in range(1, sides)
    ]
    ready = jnp.stack(query_parts, axis=1)
    ready, weight, moment, _ = lax.optimization_barrier(
        (ready, weight, moment, tokens[0, 0, :16, :128])
    )
    queries = lax.all_to_all(ready, "hd", 0, 0, tiled=True)

    gradient = head_gradient(tokens, weight)
    gradients = [gradient, lax.ppermute(gradient, "core", swap)]
    if copies > 1:
        summed = gradients[0].astype(jnp.float32) + gradients[1].astype(jnp.float32)
        gradients = [lax.psum(summed.astype(jnp.bfloat16), "rep")]
    normed = update(weight, moment, gradients, [])
    half = heads_here // 2
    near, far = tuple([*range(1, half), 0]), tuple(range(half, heads_here))
    partner = [[(c, c ^ i) for c in range(heads_here)] for i in range(heads_here)]

    columns = out_weight.shape[1]
    spans = [(0, columns // 4), (columns // 4, columns)]
    received = [[] for _ in spans]
    after, held = [], None
    for step in [*range(1, sides), 0]:
        mixed = [None] * heads_here
        for offsets in (far, near):
            applied = apply_head(queries, step, offsets, normed, after)
            after = [applied[0]]
            if held is None:
                held = hold(out_weight, out_weight_other, applied[0])
            for i, block in zip(offsets, applied):
                mixed[i] = lax.ppermute(block, "hd", partner[i]) if i else block
        if step:
            for n, span in enumerate(spans):
                partial = project(mixed, held, *span, jnp.bfloat16, after)
                after = [partial]
                partial = lax.ppermute(
                    partial, "x", [(i, (i + step) % sides) for i in range(sides)]
                )
                received[n].append(partial)
        else:
            own = project(mixed, held, 0, columns, jnp.float32, after)
    sums = [functools.reduce(jnp.add, [p.astype(jnp.float32) for p in r]) for r in received]
    return (own + jnp.concatenate(sums, axis=1)).astype(jnp.bfloat16)


def solution(mesh):
    head_axis, ctx_axis = mesh.shape["head"], mesh.shape["ctx"]

    def run(query_rows, key_rows, value_rows, token_rates, fast_weights, momentum, out_weight):
        heads_here = fast_weights.shape[0] // (head_axis // 2)
        fine = Mesh(
            mesh.devices.reshape(head_axis // 2, 2, heads_here, ctx_axis // heads_here),
            ("x", "core", "hd", "rep"),
        )
        token_spec = P(("x", "core", "hd", "rep"), None)
        weight_spec = P(("x", "core"), None, None, None)
        return jax.shard_map(
            shards,
            mesh=fine,
            in_specs=(token_spec,) * 4 + (weight_spec, weight_spec, P(("x", "core"), None)),
            out_specs=token_spec,
            check_vma=False,
        )(query_rows, key_rows, value_rows, token_rates, fast_weights, momentum, out_weight)

    return run
```

time: 190 us -> 143 us (0.75)
  waiting for transfers between devices: 87.5 us -> 48.2 us
  matrix products: 20.7 us -> 0 us
  starting transfers between devices: 23.8 us -> 37.6 us
  Pallas kernels: 22.1 us -> 35.8 us
  local copies, waits for them, and re-layouts: 23.1 us -> 9.66 us
    all_to_all x3 -> x1, waiting for transfers between devices: 46.3 us -> 7.91 us  [shards(): queries = lax.all_to_all(ready, 'hd', 0, 0, tiled=True)]
    ppermute x5 -> x20, starting transfers between devices: 3.4 us -> 24.3 us  [the longest x14 19.7 us: shards(): mixed[i] = lax.ppermute(block, 'hd', partner[i]) if i else block]
    dot_general x4 -> x0, matrix products: 20.7 us -> none  [f32_dot(): return jnp.dot(a, b, preferred_element_type=jnp.float32)]
    pallas_call x2 -> x11, Pallas kernels: 9.91 us -> 24.3 us  [the longest x1 5.78 us: hold(): pl.pallas_call(hold_kernel, in_specs=[pl.BlockSpec(memory_space=pltpu.HBM...]
    all_to_all x3 -> x1, starting transfers between devices: 11.6 us -> 4.98 us  [shards(): queries = lax.all_to_all(ready, 'hd', 0, 0, tiled=True)]
    unnamed x8, local copies, waits for them, and re-layouts: 8.23 us -> 2.1 us
    select_n x1 -> x2, other arithmetic: 2.3 us -> 7.88 us  [the longest x1 3.94 us: shards(): weight = jnp.where(owned, weight, lax.ppermute(weight, 'core', swap))]
    reshape x3 -> x0, local copies, waits for them, and re-layouts: 5.43 us -> none  [the longest x2 4.12 us: shards(): query_parts.append(part.reshape(rows, heads_here, width).transpose(1, 0, 2))]
  transfers between devices with their start and end apart: 10 -> 23, of which waited for: 6 -> 9; matrix products, arithmetic and copies ran while one was open for 19% -> 12% of each run, Pallas kernels for 12% -> 23%
where the time goes in v2:
time: 143 us
  waiting for transfers between devices  48.2 us (34%)
  starting transfers between devices  37.6 us (26%)
  Pallas kernels  35.8 us (25%)
  other arithmetic  11.2 us (8%)
  local copies, waits for them, and re-layouts  9.66 us (7%)
    ppermute x1, waiting for transfers between devices, shards(): lax.ppermute(turned[d], 'x', [(i, (i - d) % sides) for i in range(sides)])  19.8 us
    ppermute x14, starting transfers between devices, shards(): mixed[i] = lax.ppermute(block, 'hd', partner[i]) if i else block  19.7 us
    pallas_call x1, Pallas kernels, head_gradient(): pl.pallas_call(functools.partial(gradient_kernel, max(1, min(sources, 512...  11.5 us
    ppermute x14, waiting for transfers between devices, shards(): mixed[i] = lax.ppermute(block, 'hd', partner[i]) if i else block  10.7 us
    all_to_all x1, waiting for transfers between devices, shards(): queries = lax.all_to_all(ready, 'hd', 0, 0, tiled=True)  7.91 us
    all_to_all x1, starting transfers between devices, shards(): tokens = lax.all_to_all(payload, ('x', 'hd'), 0, 0, tiled=True)  7.86 us
    all_to_all x1, waiting for transfers between devices, shards(): tokens = lax.all_to_all(payload, ('x', 'hd'), 0, 0, tiled=True)  6.44 us
    pallas_call x1, Pallas kernels, hold(): pl.pallas_call(hold_kernel, in_specs=[pl.BlockSpec(memory_space=pltpu.HBM...  5.78 us
  transfers between devices with their start and end apart: 23, of which 9 were waited for; matrix products, arithmetic and copies ran while one was open for 12% of the time, Pallas kernels for 23%

profile of v2, /device:TPU:0, one launch (start us, length us, event | category | flops | bytes accessed | tf_op | source)
XLA Modules:
  0.0 142.7 jit_solution(2957689346842499302)
XLA Ops:
  1.2 4.2 %pack.1 = bf16[16,2,128,256]{3,2,1,0:T(8,128)(2,1)} custom-call(bf16[128,4096]{1,0:T(8,128)(2,1)} %key_ref.1, bf16[128,4096]{1,0:T(8,128)(2,1)} %value_ref.1, f32[16,128]{1,0:T(8,128)S(1)} %bitcast.15), custom_call_target="tpu_custom_call" | custom-call | tf_op jit(solution)/shard_map/pack/pallas_call | solution.py:42
  5.3 7.9 %all-to-all-start = ((bf16[16,2,128,256]{3,2,1,0:T(8,128)(2,1)}), bf16[16,2,128,256]{3,2,1,0:T(8,128)(2,1)S(1)}, u32[]{:S(2)}, u32[]{:S(2)}) async-start(bf16[16,2,128,256]{3,2,1,0:T(8,128)(2,1)} %pack.1), calls=%async_computation | async-start | bytes 4194304 | tf_op jit(solution)/shard_map/all_to_all | solution.py:258
  13.2 3.7 %dynamic-slice_bitcast_fusion.1 = f32[3,1024,256]{2,1,0:T(8,128)} fusion(f32[4,3,1024,256]{3,2,1,0:T(8,128)} %param.11, s32[]{:T(128)S(6)} %select_n.33), kind=kLoop, calls=%fused_computation.1 | loop fusion | bytes 6291460 | tf_op jit(solution)/shard_map/jit(dynamic_index_in_dim)/squeeze | solution.py:261
  17.2 3.7 %dynamic-slice_bitcast_fusion = f32[3,1024,256]{2,1,0:T(8,128)} fusion(f32[4,3,1024,256]{3,2,1,0:T(8,128)} %param.12, s32[]{:T(128)S(6)} %select_n.33), kind=kLoop, calls=%fused_computation | loop fusion | bytes 6291460 | tf_op jit(solution)/shard_map/jit(dynamic_index_in_dim)/squeeze | solution.py:262
  24.5 19.8 %collective-permute-done.1 = bf16[8,128,256]{2,1,0:T(8,128)(2,1)} collective-permute-done((bf16[8,128,256]{2,1,0:T(8,128)(2,1)S(1)}, bf16[8,128,256]{2,1,0:T(8,128)(2,1)}, u32[]{:S(2)}, u32[]{:S(2)}) %collective-permute-start.1) | collective-permute-done | bytes 524320 | tf_op jit(solution)/shard_map/ppermute | solution.py:269
  44.3 2.1 %pad_maximum_fusion = bf16[8,2,128,256]{3,2,1,0:T(8,128)(2,1)} fusion(bf16[8,1,128,256]{3,2,1,0:T(8,128)(2,1)} %bitcast.3, bf16[8,1,128,256]{3,2,1,0:T(8,128)(2,1)S(1)} %get-tuple-element.43), kind=kLoop, calls=%fused_computation.5 | loop fusion | flops 524288 | bytes 2097152 | tf_op jit(solution)/shard_map/stack | solution.py:272
  46.4 3.9 %broadcast_select_fusion.1.weight_ref = f32[3,1024,256]{2,1,0:T(8,128)} fusion(f32[3,1024,256]{2,1,0:T(8,128)} %collective-permute-done.2, pred[]{:T(512)S(6)} %eq.6, f32[4,3,1024,256]{3,2,1,0:T(8,128)} %param.11, s32[]{:T(128)S(6)} %select_n.33), kind=kLoop, calls=%fused_computation.4 | loop fusion | flops 786432 | bytes 9437189 | tf_op jit(solution)/shard_map/jit(_where)/select_n | solution.py:263
  50.4 3.9 %broadcast_select_fusion.momentum_ref = f32[3,1024,256]{2,1,0:T(8,128)} fusion(f32[3,1024,256]{2,1,0:T(8,128)} %collective-permute-done.3, pred[]{:T(512)S(6)} %eq.6, f32[4,3,1024,256]{3,2,1,0:T(8,128)} %param.12, s32[]{:T(128)S(6)} %select_n.33), kind=kLoop, calls=%fused_computation.3 | loop fusion | flops 786432 | bytes 9437189 | tf_op jit(solution)/shard_map/jit(_where)/select_n | solution.py:264
  54.3 6.4 %all-to-all-done.tokens_ref = bf16[16,2,128,256]{3,2,1,0:T(8,128)(2,1)S(1)} async-done(((bf16[16,2,128,256]{3,2,1,0:T(8,128)(2,1)}), bf16[16,2,128,256]{3,2,1,0:T(8,128)(2,1)S(1)}, u32[]{:S(2)}, u32[]{:S(2)}) %all-to-all-start) | async-done | bytes 2097184 | tf_op jit(solution)/shard_map/all_to_all | solution.py:258
  62.2 5.0 %all-to-all-start.1 = ((bf16[8,2,128,256]{3,2,1,0:T(8,128)(2,1)}), bf16[8,2,128,256]{3,2,1,0:T(8,128)(2,1)S(1)}, u32[]{:S(2)}, u32[]{:S(2)}) async-start(bf16[8,2,128,256]{3,2,1,0:T(8,128)(2,1)} %pad_maximum_fusion), calls=%async_computation.1 | async-start | bytes 2097152 | tf_op jit(solution)/shard_map/all_to_all | solution.py:276
  67.2 11.5 %head_gradient.1.refs_0_ = bf16[3,1024,256]{2,1,0:T(8,128)(2,1)S(1)} custom-call(bf16[16,2,128,256]{3,2,1,0:T(8,128)(2,1)} %copy-done.3, f32[3,1024,256]{2,1,0:T(8,128)} %broadcast_select_fusion.1.weight_ref), custom_call_target="tpu_custom_call" | custom-call | flops 1024 | bytes 1024 | tf_op jit(solution)/shard_map/head_gradient/pallas_call | solution.py:137
  78.8 3.4 %collective-permute-done.4.refs_1_ = bf16[3,1024,256]{2,1,0:T(8,128)(2,1)S(1)} collective-permute-done((bf16[3,1024,256]{2,1,0:T(8,128)(2,1)S(1)}, bf16[3,1024,256]{2,1,0:T(8,128)(2,1)S(1)}, u32[]{:S(2)}, u32[]{:S(2)}) %collective-permute-start.4) | collective-permute-done | bytes 1572896 | tf_op jit(solution)/shard_map/ppermute | solution.py:279
  82.2 3.0 %update.1.normed_ref = bf16[3,1024,256]{2,1,0:T(8,128)(2,1)S(1)} custom-call(f32[3,1024,256]{2,1,0:T(8,128)S(1)} %copy-done, f32[3,1024,256]{2,1,0:T(8,128)S(1)} %copy-done.1, bf16[3,1024,256]{2,1,0:T(8,128)(2,1)S(1)} %head_gradient.1.refs_0_, bf16[3,1024,256]{2,1,0:T(8,128)(2,1)S(1)} %collective-permute-done.4.refs_1_), custom_call_target="tpu_custom_call" | custom-call | flops 1024 | bytes 1024 | tf_op jit(solution)/shard_map/update/pallas_call | solution.py:177
  85.2 7.9 %all-to-all-done.1.query_ref = bf16[8,2,128,256]{3,2,1,0:T(8,128)(2,1)S(1)} async-done(((bf16[8,2,128,256]{3,2,1,0:T(8,128)(2,1)}), bf16[8,2,128,256]{3,2,1,0:T(8,128)(2,1)S(1)}, u32[]{:S(2)}, u32[]{:S(2)}) %all-to-all-start.1) | async-done | bytes 1048608 | tf_op jit(solution)/shard_map/all_to_all | solution.py:276
  97.2 2.1 %collective-permute-start.8 = (bf16[128,256]{1,0:T(8,128)(2,1)S(1)}, bf16[128,256]{1,0:T(8,128)(2,1)S(1)}, u32[]{:S(2)}, u32[]{:S(2)}) collective-permute-start(bf16[128,256]{1,0:T(8,128)(2,1)S(1)} %get-tuple-element.27.after_ref.refs_0_), channel_id=1, source_target_pairs={{0,4},{1,5},{2,6},{3,7},{4,0},{5,1},{6,2},{7,3},{8,12},{9,13},{10,... | collective-permute-start | bytes 196616 | tf_op jit(solution)/shard_map/ppermute | solution.py:300
  100.0 3.0 %collective-permute-start.9 = (bf16[128,256]{1,0:T(8,128)(2,1)S(1)}, bf16[128,256]{1,0:T(8,128)(2,1)S(1)}, u32[]{:S(2)}, u32[]{:S(2)}) collective-permute-start(bf16[128,256]{1,0:T(8,128)(2,1)S(1)} %get-tuple-element.32), channel_id=1, source_target_pairs={{0,5},{1,4},{2,7},{3,6},{4,1},{5,0},{6,3},{7,2},{8,13},{9,12},{10,... | collective-permute-start | bytes 196616 | tf_op jit(solution)/shard_map/ppermute | solution.py:300
  104.7 2.2 %collective-permute-start.11 = (bf16[128,256]{1,0:T(8,128)(2,1)S(1)}, bf16[128,256]{1,0:T(8,128)(2,1)S(1)}, u32[]{:S(2)}, u32[]{:S(2)}) collective-permute-start(bf16[128,256]{1,0:T(8,128)(2,1)S(1)} %get-tuple-element.34), channel_id=1, source_target_pairs={{0,7},{1,6},{2,5},{3,4},{4,3},{5,2},{6,1},{7,0},{8,15},{9,14},{10,... | collective-permute-start | bytes 196616 | tf_op jit(solution)/shard_map/ppermute | solution.py:300
  106.9 5.8 %hold.1.weight_ref = bf16[2048,4096]{1,0:T(8,128)(2,1)S(1)} custom-call(bf16[1024,4096]{1,0:T(8,128)(2,1)} %own_ref.1, bf16[1024,4096]{1,0:T(8,128)(2,1)} %collective-permute-done.other_ref, bf16[128,256]{1,0:T(8,128)(2,1)S(1)} %get-tuple-element.27.after_ref.refs_0_), custom_call_target="tpu_custom_call" | custom-call | flops 1024 | bytes 1024 | tf_op jit(solution)/shard_map/hold/pallas_call | solution.py:100
  121.4 2.1 %collective-permute-start.14 = (bf16[128,256]{1,0:T(8,128)(2,1)S(1)}, bf16[128,256]{1,0:T(8,128)(2,1)S(1)}, u32[]{:S(2)}, u32[]{:S(2)}) collective-permute-start(bf16[128,256]{1,0:T(8,128)(2,1)S(1)} %get-tuple-element.39), channel_id=1, source_target_pairs={{0,3},{1,2},{2,1},{3,0},{4,7},{5,6},{6,5},{7,4},{8,11},{9,10},{10,... | collective-permute-start | bytes 196616 | tf_op jit(solution)/shard_map/ppermute | solution.py:300
  124.3 2.1 %collective-permute-done.13.refs_2_ = bf16[128,256]{1,0:T(8,128)(2,1)S(1)} collective-permute-done((bf16[128,256]{1,0:T(8,128)(2,1)S(1)}, bf16[128,256]{1,0:T(8,128)(2,1)S(1)}, u32[]{:S(2)}, u32[]{:S(2)}) %collective-permute-start.13) | collective-permute-done | bytes 65568 | tf_op jit(solution)/shard_map/ppermute | solution.py:300
  129.8 2.4 %collective-permute-done.15.refs_4_ = bf16[128,256]{1,0:T(8,128)(2,1)S(1)} collective-permute-done((bf16[128,256]{1,0:T(8,128)(2,1)S(1)}, bf16[128,256]{1,0:T(8,128)(2,1)S(1)}, u32[]{:S(2)}, u32[]{:S(2)}) %collective-permute-start.15) | collective-permute-done | bytes 65568 | tf_op jit(solution)/shard_map/ppermute | solution.py:300
  132.1 2.2 %collective-permute-start.18 = (bf16[128,256]{1,0:T(8,128)(2,1)S(1)}, bf16[128,256]{1,0:T(8,128)(2,1)S(1)}, u32[]{:S(2)}, u32[]{:S(2)}) collective-permute-start(bf16[128,256]{1,0:T(8,128)(2,1)S(1)} %get-tuple-element.42), channel_id=1, source_target_pairs={{0,7},{1,6},{2,5},{3,4},{4,3},{5,2},{6,1},{7,0},{8,15},{9,14},{10,... | collective-permute-start | bytes 196616 | tf_op jit(solution)/shard_map/ppermute | solution.py:300
  134.4 4.7 %collective-permute-done.18.refs_7_ = bf16[128,256]{1,0:T(8,128)(2,1)S(1)} collective-permute-done((bf16[128,256]{1,0:T(8,128)(2,1)S(1)}, bf16[128,256]{1,0:T(8,128)(2,1)S(1)}, u32[]{:S(2)}, u32[]{:S(2)}) %collective-permute-start.18) | collective-permute-done | bytes 65568 | tf_op jit(solution)/shard_map/ppermute | solution.py:300
  139.1 2.4 %project.5 = f32[128,4096]{1,0:T(8,128)S(1)} custom-call(bf16[2048,4096]{1,0:T(8,128)(2,1)S(1)} %hold.1.weight_ref, bf16[128,256]{1,0:T(8,128)(2,1)S(1)} %get-tuple-element.36.refs_0_, bf16[128,256]{1,0:T(8,128)(2,1)S(1)} %collective-permute-done.12.refs_1_, bf16[128,256]{1,0:T(8,128)(2,1)S(1)} %collective-permute-done.13.refs_2_, ...), custom_call_target="tpu_custom_call" | custom-call | flops 1024 | bytes 1024 | tf_op jit(solution)/shard_map/project/pallas_call | solution.py:236
  (49 shorter events, 26.9 us)
Async XLA Ops:
  0.0 104.7 %collective-permute-start = (bf16[1024,4096]{1,0:T(8,128)(2,1)}, bf16[1024,4096]{1,0:T(8,128)(2,1)}, u32[]{:S(2)}, u32[]{:S(2)}) collective-permute-start(bf16[1024,4096]{1,0:T(8,128)(2,1)} %own_ref.1), channel_id=1, source_target_pairs={{0,8},{8,0},{1,9},{9,1},{2,10},{10,2},{3,11},{11,3},{4,12},{12,4},... | collective-permute-start | bytes 25165832 | tf_op jit(solution)/shard_map/ppermute | solution.py:265
  5.3 55.4 %all-to-all-start = ((bf16[16,2,128,256]{3,2,1,0:T(8,128)(2,1)}), bf16[16,2,128,256]{3,2,1,0:T(8,128)(2,1)S(1)}, u32[]{:S(2)}, u32[]{:S(2)}) async-start(bf16[16,2,128,256]{3,2,1,0:T(8,128)(2,1)} %pack.1), calls=%async_computation | async-start | bytes 4194304 | tf_op jit(solution)/shard_map/all_to_all | solution.py:258
  17.0 29.5 %collective-permute-start.2 = (f32[3,1024,256]{2,1,0:T(8,128)}, f32[3,1024,256]{2,1,0:T(8,128)}, u32[]{:S(2)}, u32[]{:S(2)}) collective-permute-start(f32[3,1024,256]{2,1,0:T(8,128)} %dynamic-slice_bitcast_fusion.1), channel_id=1, source_target_pairs={{0,8},{8,0},{1,9},{9,1},{2,10},{10,2},{3,11},{11,3},{4,12},{12,4},... | collective-permute-start | bytes 9437192 | tf_op jit(solution)/shard_map/ppermute | solution.py:263
  20.9 29.5 %collective-permute-start.3 = (f32[3,1024,256]{2,1,0:T(8,128)}, f32[3,1024,256]{2,1,0:T(8,128)}, u32[]{:S(2)}, u32[]{:S(2)}) collective-permute-start(f32[3,1024,256]{2,1,0:T(8,128)} %dynamic-slice_bitcast_fusion), channel_id=1, source_target_pairs={{0,8},{8,0},{1,9},{9,1},{2,10},{10,2},{3,11},{11,3},{4,12},{12,4},... | collective-permute-start | bytes 9437192 | tf_op jit(solution)/shard_map/ppermute | solution.py:264
  22.6 21.8 %collective-permute-start.1 = (bf16[8,128,256]{2,1,0:T(8,128)(2,1)S(1)}, bf16[8,128,256]{2,1,0:T(8,128)(2,1)}, u32[]{:S(2)}, u32[]{:S(2)}) collective-permute-start(bf16[8,128,256]{2,1,0:T(8,128)(2,1)S(1)} %get-tuple-element.44), channel_id=1, source_target_pairs={{0,16},{16,0},{1,17},{17,1},{2,18},{18,2},{3,19},{19,3},{4,20},{20... | collective-permute-start | bytes 1572872 | tf_op jit(solution)/shard_map/ppermute | solution.py:269
  62.2 31.0 %all-to-all-start.1 = ((bf16[8,2,128,256]{3,2,1,0:T(8,128)(2,1)}), bf16[8,2,128,256]{3,2,1,0:T(8,128)(2,1)S(1)}, u32[]{:S(2)}, u32[]{:S(2)}) async-start(bf16[8,2,128,256]{3,2,1,0:T(8,128)(2,1)} %pad_maximum_fusion), calls=%async_computation.1 | async-start | bytes 2097152 | tf_op jit(solution)/shard_map/all_to_all | solution.py:276
  67.1 15.0 %copy-start = (f32[3,1024,256]{2,1,0:T(8,128)S(1)}, f32[3,1024,256]{2,1,0:T(8,128)}, u32[]{:S(2)}) copy-start(f32[3,1024,256]{2,1,0:T(8,128)} %broadcast_select_fusion.1.weight_ref) | copy-start | bytes 9437188
  78.7 3.5 %collective-permute-start.4 = (bf16[3,1024,256]{2,1,0:T(8,128)(2,1)S(1)}, bf16[3,1024,256]{2,1,0:T(8,128)(2,1)S(1)}, u32[]{:S(2)}, u32[]{:S(2)}) collective-permute-start(bf16[3,1024,256]{2,1,0:T(8,128)(2,1)S(1)} %head_gradient.1.refs_0_), channel_id=1, source_target_pairs={{0,8},{8,0},{1,9},{9,1},{2,10},{10,2},{3,11},{11,3},{4,12},{12,4},... | collective-permute-start | bytes 4718600 | tf_op jit(solution)/shard_map/ppermute | solution.py:279
  95.7 4.3 %collective-permute-start.5 = (bf16[128,256]{1,0:T(8,128)(2,1)S(1)}, bf16[128,256]{1,0:T(8,128)(2,1)S(1)}, u32[]{:S(2)}, u32[]{:S(2)}) collective-permute-start(bf16[128,256]{1,0:T(8,128)(2,1)S(1)} %get-tuple-element.29.refs_8_), channel_id=1, source_target_pairs={{0,1},{1,0},{2,3},{3,2},{4,5},{5,4},{6,7},{7,6},{8,9},{9,8},{10,11... | collective-permute-start | bytes 196616 | tf_op jit(solution)/shard_map/ppermute | solution.py:300
  97.2 5.9 %collective-permute-start.6 = (bf16[128,256]{1,0:T(8,128)(2,1)S(1)}, bf16[128,256]{1,0:T(8,128)(2,1)S(1)}, u32[]{:S(2)}, u32[]{:S(2)}) collective-permute-start(bf16[128,256]{1,0:T(8,128)(2,1)S(1)} %get-tuple-element.30), channel_id=1, source_target_pairs={{0,2},{1,3},{2,0},{3,1},{4,6},{5,7},{6,4},{7,5},{8,10},{9,11},{10,... | collective-permute-start | bytes 196616 | tf_op jit(solution)/shard_map/ppermute | solution.py:300
  97.2 15.5 %collective-permute-start.8 = (bf16[128,256]{1,0:T(8,128)(2,1)S(1)}, bf16[128,256]{1,0:T(8,128)(2,1)S(1)}, u32[]{:S(2)}, u32[]{:S(2)}) collective-permute-start(bf16[128,256]{1,0:T(8,128)(2,1)S(1)} %get-tuple-element.27.after_ref.refs_0_), channel_id=1, source_target_pairs={{0,4},{1,5},{2,6},{3,7},{4,0},{5,1},{6,2},{7,3},{8,12},{9,13},{10,... | collective-permute-start | bytes 196616 | tf_op jit(solution)/shard_map/ppermute | solution.py:300
  99.2 13.5 %collective-permute-start.7 = (bf16[128,256]{1,0:T(8,128)(2,1)S(1)}, bf16[128,256]{1,0:T(8,128)(2,1)S(1)}, u32[]{:S(2)}, u32[]{:S(2)}) collective-permute-start(bf16[128,256]{1,0:T(8,128)(2,1)S(1)} %get-tuple-element.31), channel_id=1, source_target_pairs={{0,3},{1,2},{2,1},{3,0},{4,7},{5,6},{6,5},{7,4},{8,11},{9,10},{10,... | collective-permute-start | bytes 196616 | tf_op jit(solution)/shard_map/ppermute | solution.py:300
  100.0 12.7 %collective-permute-start.9 = (bf16[128,256]{1,0:T(8,128)(2,1)S(1)}, bf16[128,256]{1,0:T(8,128)(2,1)S(1)}, u32[]{:S(2)}, u32[]{:S(2)}) collective-permute-start(bf16[128,256]{1,0:T(8,128)(2,1)S(1)} %get-tuple-element.32), channel_id=1, source_target_pairs={{0,5},{1,4},{2,7},{3,6},{4,1},{5,0},{6,3},{7,2},{8,13},{9,12},{10,... | collective-permute-start | bytes 196616 | tf_op jit(solution)/shard_map/ppermute | solution.py:300
  103.0 9.7 %collective-permute-start.10 = (bf16[128,256]{1,0:T(8,128)(2,1)S(1)}, bf16[128,256]{1,0:T(8,128)(2,1)S(1)}, u32[]{:S(2)}, u32[]{:S(2)}) collective-permute-start(bf16[128,256]{1,0:T(8,128)(2,1)S(1)} %get-tuple-element.33), channel_id=1, source_target_pairs={{0,6},{1,7},{2,4},{3,5},{4,2},{5,3},{6,0},{7,1},{8,14},{9,15},{10,... | collective-permute-start | bytes 196616 | tf_op jit(solution)/shard_map/ppermute | solution.py:300
  104.7 8.0 %collective-permute-start.11 = (bf16[128,256]{1,0:T(8,128)(2,1)S(1)}, bf16[128,256]{1,0:T(8,128)(2,1)S(1)}, u32[]{:S(2)}, u32[]{:S(2)}) collective-permute-start(bf16[128,256]{1,0:T(8,128)(2,1)S(1)} %get-tuple-element.34), channel_id=1, source_target_pairs={{0,7},{1,6},{2,5},{3,4},{4,3},{5,2},{6,1},{7,0},{8,15},{9,14},{10,... | collective-permute-start | bytes 196616 | tf_op jit(solution)/shard_map/ppermute | solution.py:300
  115.3 26.2 %collective-permute-start.20 = (bf16[128,3072]{1,0:T(8,128)(2,1)S(1)}, bf16[128,3072]{1,0:T(8,128)(2,1)S(1)}, u32[]{:S(2)}, u32[]{:S(2)}) collective-permute-start(bf16[128,3072]{1,0:T(8,128)(2,1)S(1)} %project.4.refs_0_), channel_id=1, source_target_pairs={{0,16},{16,0},{1,17},{17,1},{2,18},{18,2},{3,19},{19,3},{4,20},{20... | collective-permute-start | bytes 2359304 | tf_op jit(solution)/shard_map/ppermute | solution.py:305
  116.6 24.9 %collective-permute-start.19 = (bf16[128,1024]{1,0:T(8,128)(2,1)S(1)}, bf16[128,1024]{1,0:T(8,128)(2,1)S(1)}, u32[]{:S(2)}, u32[]{:S(2)}) collective-permute-start(bf16[128,1024]{1,0:T(8,128)(2,1)S(1)} %project.3.refs_8_), channel_id=1, source_target_pairs={{0,16},{16,0},{1,17},{17,1},{2,18},{18,2},{3,19},{19,3},{4,20},{20... | collective-permute-start | bytes 786440 | tf_op jit(solution)/shard_map/ppermute | solution.py:305
  120.0 4.3 %collective-permute-start.12 = (bf16[128,256]{1,0:T(8,128)(2,1)S(1)}, bf16[128,256]{1,0:T(8,128)(2,1)S(1)}, u32[]{:S(2)}, u32[]{:S(2)}) collective-permute-start(bf16[128,256]{1,0:T(8,128)(2,1)S(1)} %get-tuple-element.37.refs_8_), channel_id=1, source_target_pairs={{0,1},{1,0},{2,3},{3,2},{4,5},{5,4},{6,7},{7,6},{8,9},{9,8},{10,11... | collective-permute-start | bytes 196616 | tf_op jit(solution)/shard_map/ppermute | solution.py:300
  121.4 5.0 %collective-permute-start.13 = (bf16[128,256]{1,0:T(8,128)(2,1)S(1)}, bf16[128,256]{1,0:T(8,128)(2,1)S(1)}, u32[]{:S(2)}, u32[]{:S(2)}) collective-permute-start(bf16[128,256]{1,0:T(8,128)(2,1)S(1)} %get-tuple-element.38), channel_id=1, source_target_pairs={{0,2},{1,3},{2,0},{3,1},{4,6},{5,7},{6,4},{7,5},{8,10},{9,11},{10,... | collective-permute-start | bytes 196616 | tf_op jit(solution)/shard_map/ppermute | solution.py:300
  121.4 6.6 %collective-permute-start.14 = (bf16[128,256]{1,0:T(8,128)(2,1)S(1)}, bf16[128,256]{1,0:T(8,128)(2,1)S(1)}, u32[]{:S(2)}, u32[]{:S(2)}) collective-permute-start(bf16[128,256]{1,0:T(8,128)(2,1)S(1)} %get-tuple-element.39), channel_id=1, source_target_pairs={{0,3},{1,2},{2,1},{3,0},{4,7},{5,6},{6,5},{7,4},{8,11},{9,10},{10,... | collective-permute-start | bytes 196616 | tf_op jit(solution)/shard_map/ppermute | solution.py:300
  124.3 7.9 %collective-permute-start.15 = (bf16[128,256]{1,0:T(8,128)(2,1)S(1)}, bf16[128,256]{1,0:T(8,128)(2,1)S(1)}, u32[]{:S(2)}, u32[]{:S(2)}) collective-permute-start(bf16[128,256]{1,0:T(8,128)(2,1)S(1)} %get-tuple-element.35.refs_0_), channel_id=1, source_target_pairs={{0,4},{1,5},{2,6},{3,7},{4,0},{5,1},{6,2},{7,3},{8,12},{9,13},{10,... | collective-permute-start | bytes 196616 | tf_op jit(solution)/shard_map/ppermute | solution.py:300
  126.4 8.0 %collective-permute-start.16 = (bf16[128,256]{1,0:T(8,128)(2,1)S(1)}, bf16[128,256]{1,0:T(8,128)(2,1)S(1)}, u32[]{:S(2)}, u32[]{:S(2)}) collective-permute-start(bf16[128,256]{1,0:T(8,128)(2,1)S(1)} %get-tuple-element.40), channel_id=1, source_target_pairs={{0,5},{1,4},{2,7},{3,6},{4,1},{5,0},{6,3},{7,2},{8,13},{9,12},{10,... | collective-permute-start | bytes 196616 | tf_op jit(solution)/shard_map/ppermute | solution.py:300
  128.1 6.3 %collective-permute-start.17 = (bf16[128,256]{1,0:T(8,128)(2,1)S(1)}, bf16[128,256]{1,0:T(8,128)(2,1)S(1)}, u32[]{:S(2)}, u32[]{:S(2)}) collective-permute-start(bf16[128,256]{1,0:T(8,128)(2,1)S(1)} %get-tuple-element.41), channel_id=1, source_target_pairs={{0,6},{1,7},{2,4},{3,5},{4,2},{5,3},{6,0},{7,1},{8,14},{9,15},{10,... | collective-permute-start | bytes 196616 | tf_op jit(solution)/shard_map/ppermute | solution.py:300
  132.1 7.0 %collective-permute-start.18 = (bf16[128,256]{1,0:T(8,128)(2,1)S(1)}, bf16[128,256]{1,0:T(8,128)(2,1)S(1)}, u32[]{:S(2)}, u32[]{:S(2)}) collective-permute-start(bf16[128,256]{1,0:T(8,128)(2,1)S(1)} %get-tuple-element.42), channel_id=1, source_target_pairs={{0,7},{1,6},{2,5},{3,4},{4,3},{5,2},{6,1},{7,0},{8,15},{9,14},{10,... | collective-permute-start | bytes 196616 | tf_op jit(solution)/shard_map/ppermute | solution.py:300
  (3 other events, 17.1 us)

commit v3 on v2

--- a/solution.py
+++ b/solution.py
@@ -9,7 +9,7 @@
 from jax.sharding import PartitionSpec as P
 
 NT = (((1,), (1,)), ((), ()))
-VMEM = 14 << 20
+VMEM = 24 << 20
 SMALL = pl.CostEstimate(flops=1024, bytes_accessed=1024, transcendentals=0)
 
 
@@ -51,7 +51,12 @@
         out_shape=jax.ShapeDtypeStruct((heads, 2, rows, width), key_rows.dtype),
         compiler_params=pltpu.CompilerParams(vmem_limit_bytes=VMEM),
         name="pack",
-    )(*(pltpu.with_memory_space_constraint(a, pltpu.HBM) for a in (key_rows, value_rows)), token_rates.T)
+    )(
+        *(
+            pltpu.with_memory_space_constraint(a, pltpu.HBM)
+            for a in (key_rows, value_rows, token_rates.T)
+        )
+    )
 
 
 def turn_kernel(side_ref, rows_ref, out_ref):
@@ -80,28 +85,30 @@
     )(side[None], pltpu.with_memory_space_constraint(query_rows, pltpu.HBM))
 
 
-def hold_kernel(own_ref, other_ref, after_ref, out_ref, sems):
+def hold_kernel(start, own_ref, other_ref, after_ref, out_ref, sems):
     core = lax.axis_index("core")
-    depth = own_ref.shape[0]
-    first = pltpu.make_async_copy(own_ref, out_ref.at[pl.ds(core * depth, depth)], sems.at[0])
-    second = pltpu.make_async_copy(
-        other_ref, out_ref.at[pl.ds((1 - core) * depth, depth)], sems.at[1]
-    )
-    first.start()
-    second.start()
-    first.wait()
-    second.wait()
-
-
-def hold(own, other, after):
-    depth, columns = own.shape
+    depth, count = own_ref.shape[0], out_ref.shape[1]
+    copies = [
+        pltpu.make_async_copy(
+            ref.at[:, pl.ds(start, count)], out_ref.at[pl.ds(place * depth, depth)], sems.at[n]
+        )
+        for n, (ref, place) in enumerate(((own_ref, core), (other_ref, 1 - core)))
+    ]
+    for copy in copies:
+        copy.start()
+    for copy in copies:
+        copy.wait()
+
+
+def hold(own, other, start, stop, after):
+    depth = own.shape[0]
     own = pltpu.with_memory_space_constraint(own, pltpu.HBM)
     other = pltpu.with_memory_space_constraint(other, pltpu.HBM)
     return pl.pallas_call(
-        hold_kernel,
+        functools.partial(hold_kernel, start),
         in_specs=[pl.BlockSpec(memory_space=pltpu.HBM)] * 2 + [pl.BlockSpec(memory_space=pl.ANY)],
         out_specs=pl.BlockSpec(memory_space=pltpu.VMEM),
-        out_shape=pltpu.VMEM((2 * depth, columns), own.dtype),
+        out_shape=pltpu.VMEM((2 * depth, stop - start), own.dtype),
         scratch_shapes=[pltpu.SemaphoreType.DMA((2,))],
         compiler_params=pltpu.CompilerParams(vmem_limit_bytes=VMEM),
         cost_estimate=SMALL,
@@ -146,7 +153,7 @@
         compiler_params=pltpu.CompilerParams(vmem_limit_bytes=VMEM),
         cost_estimate=SMALL,
         name="head_gradient",
-    )(*(pltpu.with_memory_space_constraint(a, pltpu.HBM) for a in (tokens, weight)))
+    )(tokens, pltpu.with_memory_space_constraint(weight, pltpu.HBM))
 
 
 def update_kernel(terms, weight_ref, momentum_ref, *refs):
@@ -186,63 +193,73 @@
     )(weight, moment, *gradients, *after)
 
 
-def apply_kernel(part, offsets, normed_ref, query_ref, *refs):
+def apply_kernel(parts, offsets, normed_ref, query_ref, *refs):
     out_refs = refs[-len(offsets) :]
     head = lax.axis_index("hd")
     _, _, rows, _ = query_ref.shape
     group = max(1, min(len(offsets), 512 // rows))
-    for start in range(0, len(offsets), group):
-        picked = offsets[start : start + group]
-        query = jnp.concatenate([query_ref[jnp.bitwise_xor(head, i), part] for i in picked], axis=0)
-        pre = lax.dot_general(query, normed_ref[0], NT, preferred_element_type=jnp.float32)
-        gate = lax.dot_general(query, normed_ref[1], NT, preferred_element_type=jnp.float32)
-        hidden = (pre * sigmoid(pre) * gate).astype(jnp.bfloat16)
-        out = f32_dot(hidden, normed_ref[2]).astype(jnp.bfloat16)
-        for n in range(len(picked)):
-            out_refs[start + n][...] = out[n * rows : (n + 1) * rows]
-
-
-def apply_head(queries, part, offsets, normed, after):
+    for p, part in enumerate(parts):
+        for start in range(0, len(offsets), group):
+            picked = offsets[start : start + group]
+            query = jnp.concatenate(
+                [query_ref[jnp.bitwise_xor(head, i), part] for i in picked], axis=0
+            )
+            pre = lax.dot_general(query, normed_ref[0], NT, preferred_element_type=jnp.float32)
+            gate = lax.dot_general(query, normed_ref[1], NT, preferred_element_type=jnp.float32)
+            hidden = (pre * sigmoid(pre) * gate).astype(jnp.bfloat16)
+            out = f32_dot(hidden, normed_ref[2]).astype(jnp.bfloat16)
+            for n in range(len(picked)):
+                out_refs[start + n][p] = out[n * rows : (n + 1) * rows]
+
+
+def apply_head(queries, parts, offsets, normed, after):
     _, _, rows, width = queries.shape
     whole = pl.BlockSpec(memory_space=pltpu.VMEM)
-    return pl.pallas_call(
-        functools.partial(apply_kernel, part, offsets),
+    shape = jax.ShapeDtypeStruct((len(parts), rows, width), jnp.bfloat16)
+    return pl.pallas_call(
+        functools.partial(apply_kernel, parts, offsets),
         in_specs=[whole, whole] + [pl.BlockSpec(memory_space=pl.ANY)] * len(after),
         out_specs=[whole] * len(offsets),
-        out_shape=[jax.ShapeDtypeStruct((rows, width), jnp.bfloat16)] * len(offsets),
+        out_shape=[shape] * len(offsets),
         compiler_params=pltpu.CompilerParams(vmem_limit_bytes=VMEM),
         cost_estimate=SMALL,
         name="apply_head",
     )(normed, queries, *after)
 
 
-def project_kernel(block, start, terms, weight_ref, *refs):
+def project_kernel(places, pieces, *refs):
+    terms = len(places)
     mixed_refs, out_ref, depth_ref = refs[:terms], refs[-2], refs[-1]
     head = lax.axis_index("hd")
-    rows, width = mixed_refs[0].shape
-    for i, ref in enumerate(mixed_refs):
-        depth_ref[jnp.bitwise_xor(head, i)] = ref[...]
-    mixed = jnp.concatenate([depth_ref[i] for i in range(len(mixed_refs))], axis=1)
-    for first in range(0, out_ref.shape[1], block):
-        part = f32_dot(mixed, weight_ref[:, start + first : start + first + block])
-        out_ref[:, first : first + block] = part.astype(out_ref.dtype)
-
-
-def project(mixed, weight, start, stop, dtype, after):
-    rows, width = mixed[0].shape
-    block = min(512, stop - start)
+    for i, (ref, place) in enumerate(zip(mixed_refs, places)):
+        depth_ref[jnp.bitwise_xor(head, i)] = ref[place]
+    mixed = jnp.concatenate([depth_ref[i] for i in range(terms)], axis=1)
+    first = 0
+    for weight_ref in refs[terms : terms + pieces]:
+        columns = weight_ref.shape[1]
+        block = 512 if columns % 512 == 0 else columns
+        for start in range(0, columns, block):
+            part = f32_dot(mixed, weight_ref[:, start : start + block])
+            out_ref[:, first + start : first + start + block] = part.astype(out_ref.dtype)
+        first += columns
+
+
+def project(blocks, weights, dtype, after):
+    mixed, places = zip(*blocks)
+    _, rows, width = mixed[0].shape
     whole = pl.BlockSpec(memory_space=pltpu.VMEM)
-    weight = pltpu.with_memory_space_constraint(weight, pltpu.VMEM)
-    return pl.pallas_call(
-        functools.partial(project_kernel, block, start, len(mixed)),
-        in_specs=[whole] * (1 + len(mixed)) + [pl.BlockSpec(memory_space=pl.ANY)] * len(after),
+    weights = [pltpu.with_memory_space_constraint(w, pltpu.VMEM) for w in weights]
+    return pl.pallas_call(
+        functools.partial(project_kernel, places, len(weights)),
+        in_specs=[whole] * (len(mixed) + len(weights))
+        + [pl.BlockSpec(memory_space=pl.ANY)] * len(after),
         out_specs=whole,
-        out_shape=jax.ShapeDtypeStruct((rows, stop - start), dtype),
+        out_shape=jax.ShapeDtypeStruct((rows, sum(w.shape[1] for w in weights)), dtype),
         scratch_shapes=[pltpu.VMEM((len(mixed), rows, width), mixed[0].dtype)],
         compiler_params=pltpu.CompilerParams(vmem_limit_bytes=VMEM),
         cost_estimate=SMALL,
         name="project",
-    )(weight, *mixed, *after)
+    )(*mixed, *weights, *after)
 
 
 def shards(query_rows, key_rows, value_rows, token_rates, fast_weights, momentum, out_weight):
@@ -270,9 +287,7 @@
         for d in range(1, sides)
     ]
     ready = jnp.stack(query_parts, axis=1)
-    ready, weight, moment, _ = lax.optimization_barrier(
-        (ready, weight, moment, tokens[0, 0, :16, :128])
-    )
+    ready, weight, moment, tokens = lax.optimization_barrier((ready, weight, moment, tokens))
     queries = lax.all_to_all(ready, "hd", 0, 0, tiled=True)
 
     gradient = head_gradient(tokens, weight)
@@ -286,28 +301,41 @@
     partner = [[(c, c ^ i) for c in range(heads_here)] for i in range(heads_here)]
 
     columns = out_weight.shape[1]
-    spans = [(0, columns // 4), (columns // 4, columns)]
-    received = [[] for _ in spans]
-    after, held = [], None
-    for step in [*range(1, sides), 0]:
-        mixed = [None] * heads_here
-        for offsets in (far, near):
-            applied = apply_head(queries, step, offsets, normed, after)
-            after = [applied[0]]
-            if held is None:
-                held = hold(out_weight, out_weight_other, applied[0])
-            for i, block in zip(offsets, applied):
-                mixed[i] = lax.ppermute(block, "hd", partner[i]) if i else block
+    split = columns * 3 // 4
+    steps = (*range(1, sides), 0)
+
+    def spread(parts, offsets, after):
+        applied = apply_head(queries, parts, offsets, normed, after)
+        moved = [
+            lax.ppermute(block, "hd", partner[i]) if i else block
+            for i, block in zip(offsets, applied)
+        ]
+        return moved, applied[0]
+
+    crossing, done = {}, None
+    crossing[steps[0]], done = spread(steps[:1], far, [])
+    local, done = spread(steps, near, [done])
+    held = [hold(out_weight, out_weight_other, 0, split, done)]
+    crossing[steps[1]], done = spread(steps[1:2], far, held)
+    received = [[], []]
+    for place, step in enumerate(steps):
+        if step not in crossing:
+            crossing[step], done = spread((step,), far, [done])
+        blocks = [None] * heads_here
+        for i, block in zip(near, local):
+            blocks[i] = (block, place)
+        for i, block in zip(far, crossing[step]):
+            blocks[i] = (block, 0)
         if step:
-            for n, span in enumerate(spans):
-                partial = project(mixed, held, *span, jnp.bfloat16, after)
-                after = [partial]
-                partial = lax.ppermute(
-                    partial, "x", [(i, (i + step) % sides) for i in range(sides)]
-                )
-                received[n].append(partial)
+            over = [(i, (i + step) % sides) for i in range(sides)]
+            done = project(blocks, held[:1], jnp.bfloat16, [done])
+            received[0].append(lax.ppermute(done, "x", over))
+            if len(held) == 1:
+                held.append(hold(out_weight, out_weight_other, split, columns, done))
+            done = project(blocks, held[1:], jnp.bfloat16, [])
+            received[1].append(lax.ppermute(done, "x", over))
         else:
-            own = project(mixed, held, 0, columns, jnp.float32, after)
+            own = project(blocks, held, jnp.float32, [])
     sums = [functools.reduce(jnp.add, [p.astype(jnp.float32) for p in r]) for r in received]
     return (own + jnp.concatenate(sums, axis=1)).astype(jnp.bfloat16)
 

time: 143 us -> 140 us (0.979)
  starting transfers between devices: 37.6 us -> 33.9 us
  local copies, waits for them, and re-layouts: 9.66 us -> 11.9 us
    ppermute x16 -> x13, starting transfers between devices: 21.8 us -> 18.1 us  [the longest x11 16 us: spread(): lax.ppermute(block, 'hd', partner[i])]
    unnamed x8 -> x10, local copies, waits for them, and re-layouts: 2.1 us -> 4.36 us
    ppermute x16 -> x13, waiting for transfers between devices: 10.7 us -> 10.7 us  [the longest x11 8.64 us: spread(): lax.ppermute(block, 'hd', partner[i])]
  transfers between devices with their start and end apart: 23 -> 20, of which waited for: 9 -> 9; matrix products, arithmetic and copies ran while one was open for 12% -> 13% of each run, Pallas kernels for 23% -> 23%
where the time goes in v3:
time: 140 us; the launch traced here: 139 us
  waiting for transfers between devices  47.4 us (34%)
  Pallas kernels  34.4 us (25%)
  starting transfers between devices  33.9 us (24%)
  local copies, waits for them, and re-layouts  11.9 us (8%)
  other arithmetic  11.2 us (8%)
    ppermute x1, waiting for transfers between devices, shards(): lax.ppermute(turned[d], 'x', [(i, (i - d) % sides) for i in range(sides)])  19.8 us
    ppermute x11, starting transfers between devices, spread(): lax.ppermute(block, 'hd', partner[i])  16 us
    pallas_call x1, Pallas kernels, head_gradient(): pl.pallas_call(functools.partial(gradient_kernel, max(1, min(sources, 512...  10.8 us
    ppermute x11, waiting for transfers between devices, spread(): lax.ppermute(block, 'hd', partner[i])  8.64 us
    all_to_all x1, starting transfers between devices, shards(): tokens = lax.all_to_all(payload, ('x', 'hd'), 0, 0, tiled=True)  7.87 us
    all_to_all x1, waiting for transfers between devices, shards(): queries = lax.all_to_all(ready, 'hd', 0, 0, tiled=True)  7.07 us
    pallas_call x2, Pallas kernels, hold(): pl.pallas_call(functools.partial(hold_kernel, start), in_specs=[pl.BlockS...  6.87 us
    all_to_all x1, waiting for transfers between devices, shards(): tokens = lax.all_to_all(payload, ('x', 'hd'), 0, 0, tiled=True)  6.45 us
  transfers between devices with their start and end apart: 20, of which 9 were waited for; matrix products, arithmetic and copies ran while one was open for 13% of the time, Pallas kernels for 23%

profile of v3, /device:TPU:0, one launch (start us, length us, event | category | flops | bytes accessed | tf_op | source)
XLA Modules:
  0.0 139.0 jit_solution(396860924580153547)
XLA Ops:
  0.5 2.9 %pack.1 = bf16[16,2,128,256]{3,2,1,0:T(8,128)(2,1)S(1)} custom-call(bf16[128,4096]{1,0:T(8,128)(2,1)} %key_ref.1, bf16[128,4096]{1,0:T(8,128)(2,1)} %value_ref.1, f32[16,128]{1,0:T(8,128)} %bitcast.15), custom_call_target="tpu_custom_call" | custom-call | tf_op jit(solution)/shard_map/pack/pallas_call | solution.py:42
  4.7 7.9 %all-to-all-start = ((bf16[16,2,128,256]{3,2,1,0:T(8,128)(2,1)}), bf16[16,2,128,256]{3,2,1,0:T(8,128)(2,1)S(1)}, u32[]{:S(2)}, u32[]{:S(2)}) async-start(bf16[16,2,128,256]{3,2,1,0:T(8,128)(2,1)} %copy-done.4), calls=%async_computation | async-start | bytes 4194304 | tf_op jit(solution)/shard_map/all_to_all | solution.py:275
  12.6 3.7 %dynamic-slice_bitcast_fusion = f32[3,1024,256]{2,1,0:T(8,128)} fusion(f32[4,3,1024,256]{3,2,1,0:T(8,128)} %param.12, s32[]{:T(128)S(6)} %select_n.33), kind=kLoop, calls=%fused_computation | loop fusion | bytes 6291460 | tf_op jit(solution)/shard_map/jit(dynamic_index_in_dim)/squeeze | solution.py:279
  16.6 3.7 %dynamic-slice_bitcast_fusion.1 = f32[3,1024,256]{2,1,0:T(8,128)} fusion(f32[4,3,1024,256]{3,2,1,0:T(8,128)} %param.11, s32[]{:T(128)S(6)} %select_n.33), kind=kLoop, calls=%fused_computation.1 | loop fusion | bytes 6291460 | tf_op jit(solution)/shard_map/jit(dynamic_index_in_dim)/squeeze | solution.py:278
  23.9 19.8 %collective-permute-done = bf16[8,128,256]{2,1,0:T(8,128)(2,1)} collective-permute-done((bf16[8,128,256]{2,1,0:T(8,128)(2,1)S(1)}, bf16[8,128,256]{2,1,0:T(8,128)(2,1)}, u32[]{:S(2)}, u32[]{:S(2)}) %collective-permute-start) | collective-permute-done | bytes 524320 | tf_op jit(solution)/shard_map/ppermute | solution.py:286
  43.7 2.1 %pad_maximum_fusion = bf16[8,2,128,256]{3,2,1,0:T(8,128)(2,1)} fusion(bf16[8,1,128,256]{3,2,1,0:T(8,128)(2,1)} %bitcast.3, bf16[8,1,128,256]{3,2,1,0:T(8,128)(2,1)S(1)} %get-tuple-element.37), kind=kLoop, calls=%fused_computation.5 | loop fusion | flops 524288 | bytes 2097152 | tf_op jit(solution)/shard_map/stack | solution.py:289
  45.8 3.9 %broadcast_select_fusion.momentum_ref = f32[3,1024,256]{2,1,0:T(8,128)} fusion(f32[3,1024,256]{2,1,0:T(8,128)} %collective-permute-done.2, pred[]{:T(512)S(6)} %eq.6, f32[4,3,1024,256]{3,2,1,0:T(8,128)} %param.12, s32[]{:T(128)S(6)} %select_n.33), kind=kLoop, calls=%fused_computation.3 | loop fusion | flops 786432 | bytes 9437189 | tf_op jit(solution)/shard_map/jit(_where)/select_n | solution.py:281
  49.8 3.9 %broadcast_select_fusion.1.weight_ref = f32[3,1024,256]{2,1,0:T(8,128)} fusion(f32[3,1024,256]{2,1,0:T(8,128)} %collective-permute-done.1, pred[]{:T(512)S(6)} %eq.6, f32[4,3,1024,256]{3,2,1,0:T(8,128)} %param.11, s32[]{:T(128)S(6)} %select_n.33), kind=kLoop, calls=%fused_computation.4 | loop fusion | flops 786432 | bytes 9437189 | tf_op jit(solution)/shard_map/jit(_where)/select_n | solution.py:280
  53.7 6.4 %all-to-all-done.tokens_ref = bf16[16,2,128,256]{3,2,1,0:T(8,128)(2,1)S(1)} async-done(((bf16[16,2,128,256]{3,2,1,0:T(8,128)(2,1)}), bf16[16,2,128,256]{3,2,1,0:T(8,128)(2,1)S(1)}, u32[]{:S(2)}, u32[]{:S(2)}) %all-to-all-start) | async-done | bytes 2097184 | tf_op jit(solution)/shard_map/all_to_all | solution.py:275
  61.6 4.9 %all-to-all-start.1 = ((bf16[8,2,128,256]{3,2,1,0:T(8,128)(2,1)}), bf16[8,2,128,256]{3,2,1,0:T(8,128)(2,1)S(1)}, u32[]{:S(2)}, u32[]{:S(2)}) async-start(bf16[8,2,128,256]{3,2,1,0:T(8,128)(2,1)} %pad_maximum_fusion), calls=%async_computation.1 | async-start | bytes 2097152 | tf_op jit(solution)/shard_map/all_to_all | solution.py:291
  68.1 10.8 %head_gradient.1.refs_0_ = bf16[3,1024,256]{2,1,0:T(8,128)(2,1)S(1)} custom-call(bf16[16,2,128,256]{3,2,1,0:T(8,128)(2,1)S(1)} %copy-done.3, f32[3,1024,256]{2,1,0:T(8,128)} %broadcast_select_fusion.1.weight_ref), custom_call_target="tpu_custom_call" | custom-call | flops 1024 | bytes 1024 | tf_op jit(solution)/shard_map/head_gradient/pallas_call | solution.py:144
  79.0 3.4 %collective-permute-done.3.refs_1_ = bf16[3,1024,256]{2,1,0:T(8,128)(2,1)S(1)} collective-permute-done((bf16[3,1024,256]{2,1,0:T(8,128)(2,1)S(1)}, bf16[3,1024,256]{2,1,0:T(8,128)(2,1)S(1)}, u32[]{:S(2)}, u32[]{:S(2)}) %collective-permute-start.3) | collective-permute-done | bytes 1572896 | tf_op jit(solution)/shard_map/ppermute | solution.py:294
  82.4 3.0 %update.1.normed_ref = bf16[3,1024,256]{2,1,0:T(8,128)(2,1)S(1)} custom-call(f32[3,1024,256]{2,1,0:T(8,128)S(1)} %copy-done, f32[3,1024,256]{2,1,0:T(8,128)S(1)} %copy-done.1, bf16[3,1024,256]{2,1,0:T(8,128)(2,1)S(1)} %head_gradient.1.refs_0_, bf16[3,1024,256]{2,1,0:T(8,128)(2,1)S(1)} %collective-permute-done.3.refs_1_), custom_call_target="tpu_custom_call" | custom-call | flops 1024 | bytes 1024 | tf_op jit(solution)/shard_map/update/pallas_call | solution.py:184
  85.4 7.1 %all-to-all-done.1.query_ref = bf16[8,2,128,256]{3,2,1,0:T(8,128)(2,1)S(1)} async-done(((bf16[8,2,128,256]{3,2,1,0:T(8,128)(2,1)}), bf16[8,2,128,256]{3,2,1,0:T(8,128)(2,1)S(1)}, u32[]{:S(2)}, u32[]{:S(2)}) %all-to-all-start.1) | async-done | bytes 1048608 | tf_op jit(solution)/shard_map/all_to_all | solution.py:291
  97.9 2.4 %collective-permute-start.5 = (bf16[2,128,256]{2,1,0:T(8,128)(2,1)S(1)}, bf16[2,128,256]{2,1,0:T(8,128)(2,1)S(1)}, u32[]{:S(2)}, u32[]{:S(2)}) collective-permute-start(bf16[2,128,256]{2,1,0:T(8,128)(2,1)S(1)} %get-tuple-element.28), channel_id=1, source_target_pairs={{0,2},{1,3},{2,0},{3,1},{4,6},{5,7},{6,4},{7,5},{8,10},{9,11},{10,... | collective-permute-start | bytes 393224 | tf_op jit(solution)/shard_map/ppermute | solution.py:310
  102.8 2.3 %collective-permute-start.15 = (bf16[1,128,256]{2,1,0:T(8,128)(2,1)S(1)}, bf16[1,128,256]{2,1,0:T(8,128)(2,1)S(1)}, u32[]{:S(2)}, u32[]{:S(2)}) collective-permute-start(bf16[1,128,256]{2,1,0:T(8,128)(2,1)S(1)} %get-tuple-element.36), channel_id=1, source_target_pairs={{0,7},{1,6},{2,5},{3,4},{4,3},{5,2},{6,1},{7,0},{8,15},{9,14},{10,... | collective-permute-start | bytes 196616 | tf_op jit(solution)/shard_map/ppermute | solution.py:310
  105.3 4.6 %hold.2.refs_0_.refs_8_ = bf16[2048,3072]{1,0:T(8,128)(2,1)S(1)} custom-call(bf16[1024,4096]{1,0:T(8,128)(2,1)} %own_ref.3, bf16[1024,4096]{1,0:T(8,128)(2,1)} %collective-permute-done.7.other_ref, bf16[2,128,256]{2,1,0:T(8,128)(2,1)S(1)} %get-tuple-element.27.after_ref), custom_call_target="tpu_custom_call" | custom-call | flops 1024 | bytes 1024 | tf_op jit(solution)/shard_map/hold/pallas_call | solution.py:107
  114.4 2.2 %hold.3.refs_9_.refs_8_ = bf16[2048,1024]{1,0:T(8,128)(2,1)S(1)} custom-call(bf16[1024,4096]{1,0:T(8,128)(2,1)} %own_ref.3, bf16[1024,4096]{1,0:T(8,128)(2,1)} %collective-permute-done.7.other_ref, bf16[128,3072]{1,0:T(8,128)(2,1)S(1)} %project.3.after_ref), custom_call_target="tpu_custom_call" | custom-call | flops 1024 | bytes 1024 | tf_op jit(solution)/shard_map/hold/pallas_call | solution.py:107
  118.3 3.2 %collective-permute-start.9 = (bf16[1,128,256]{2,1,0:T(8,128)(2,1)S(1)}, bf16[1,128,256]{2,1,0:T(8,128)(2,1)S(1)}, u32[]{:S(2)}, u32[]{:S(2)}) collective-permute-start(bf16[1,128,256]{2,1,0:T(8,128)(2,1)S(1)} %get-tuple-element.31), channel_id=1, source_target_pairs={{0,5},{1,4},{2,7},{3,6},{4,1},{5,0},{6,3},{7,2},{8,13},{9,12},{10,... | collective-permute-start | bytes 196616 | tf_op jit(solution)/shard_map/ppermute | solution.py:310
  123.4 2.3 %collective-permute-start.11 = (bf16[1,128,256]{2,1,0:T(8,128)(2,1)S(1)}, bf16[1,128,256]{2,1,0:T(8,128)(2,1)S(1)}, u32[]{:S(2)}, u32[]{:S(2)}) collective-permute-start(bf16[1,128,256]{2,1,0:T(8,128)(2,1)S(1)} %get-tuple-element.33), channel_id=1, source_target_pairs={{0,7},{1,6},{2,5},{3,4},{4,3},{5,2},{6,1},{7,0},{8,15},{9,14},{10,... | collective-permute-start | bytes 196616 | tf_op jit(solution)/shard_map/ppermute | solution.py:310
  125.7 2.5 %collective-permute-done.9.refs_5_ = bf16[1,128,256]{2,1,0:T(8,128)(2,1)S(1)} collective-permute-done((bf16[1,128,256]{2,1,0:T(8,128)(2,1)S(1)}, bf16[1,128,256]{2,1,0:T(8,128)(2,1)S(1)}, u32[]{:S(2)}, u32[]{:S(2)}) %collective-permute-start.9) | collective-permute-done | bytes 65568 | tf_op jit(solution)/shard_map/ppermute | solution.py:310
  128.2 2.2 %collective-permute-done.11.refs_7_ = bf16[1,128,256]{2,1,0:T(8,128)(2,1)S(1)} collective-permute-done((bf16[1,128,256]{2,1,0:T(8,128)(2,1)S(1)}, bf16[1,128,256]{2,1,0:T(8,128)(2,1)S(1)}, u32[]{:S(2)}, u32[]{:S(2)}) %collective-permute-start.11) | collective-permute-done | bytes 65568 | tf_op jit(solution)/shard_map/ppermute | solution.py:310
  130.4 3.0 %collective-permute-done.8.refs_4_ = bf16[1,128,256]{2,1,0:T(8,128)(2,1)S(1)} collective-permute-done((bf16[1,128,256]{2,1,0:T(8,128)(2,1)S(1)}, bf16[1,128,256]{2,1,0:T(8,128)(2,1)S(1)}, u32[]{:S(2)}, u32[]{:S(2)}) %collective-permute-start.8) | collective-permute-done | bytes 65568 | tf_op jit(solution)/shard_map/ppermute | solution.py:310
  133.4 2.4 %project.4 = f32[128,4096]{1,0:T(8,128)S(1)} custom-call(bf16[2,128,256]{2,1,0:T(8,128)(2,1)S(1)} %get-tuple-element.26.refs_0_, bf16[2,128,256]{2,1,0:T(8,128)(2,1)S(1)} %collective-permute-done.4.refs_1_, bf16[2,128,256]{2,1,0:T(8,128)(2,1)S(1)} %collective-permute-done.5.refs_2_, bf16[2,128,256]{2,1,0:T(8,128)(2,1)S(1)} %collective-permute-done.6.refs_3_, ...), custom_call_target="tpu_custom_call" | custom-call | flops 1024 | bytes 1024 | tf_op jit(solution)/shard_map/project/pallas_call | solution.py:252
  (45 shorter events, 27.9 us)
Async XLA Ops:
  0.0 105.1 %collective-permute-start.7 = (bf16[1024,4096]{1,0:T(8,128)(2,1)}, bf16[1024,4096]{1,0:T(8,128)(2,1)}, u32[]{:S(2)}, u32[]{:S(2)}) collective-permute-start(bf16[1024,4096]{1,0:T(8,128)(2,1)} %own_ref.3), channel_id=1, source_target_pairs={{0,8},{8,0},{1,9},{9,1},{2,10},{10,2},{3,11},{11,3},{4,12},{12,4},... | collective-permute-start | bytes 25165832 | tf_op jit(solution)/shard_map/ppermute | solution.py:282
  4.7 55.4 %all-to-all-start = ((bf16[16,2,128,256]{3,2,1,0:T(8,128)(2,1)}), bf16[16,2,128,256]{3,2,1,0:T(8,128)(2,1)S(1)}, u32[]{:S(2)}, u32[]{:S(2)}) async-start(bf16[16,2,128,256]{3,2,1,0:T(8,128)(2,1)} %copy-done.4), calls=%async_computation | async-start | bytes 4194304 | tf_op jit(solution)/shard_map/all_to_all | solution.py:275
  16.4 29.5 %collective-permute-start.2 = (f32[3,1024,256]{2,1,0:T(8,128)}, f32[3,1024,256]{2,1,0:T(8,128)}, u32[]{:S(2)}, u32[]{:S(2)}) collective-permute-start(f32[3,1024,256]{2,1,0:T(8,128)} %dynamic-slice_bitcast_fusion), channel_id=1, source_target_pairs={{0,8},{8,0},{1,9},{9,1},{2,10},{10,2},{3,11},{11,3},{4,12},{12,4},... | collective-permute-start | bytes 9437192 | tf_op jit(solution)/shard_map/ppermute | solution.py:281
  20.3 29.5 %collective-permute-start.1 = (f32[3,1024,256]{2,1,0:T(8,128)}, f32[3,1024,256]{2,1,0:T(8,128)}, u32[]{:S(2)}, u32[]{:S(2)}) collective-permute-start(f32[3,1024,256]{2,1,0:T(8,128)} %dynamic-slice_bitcast_fusion.1), channel_id=1, source_target_pairs={{0,8},{8,0},{1,9},{9,1},{2,10},{10,2},{3,11},{11,3},{4,12},{12,4},... | collective-permute-start | bytes 9437192 | tf_op jit(solution)/shard_map/ppermute | solution.py:280
  21.9 21.8 %collective-permute-start = (bf16[8,128,256]{2,1,0:T(8,128)(2,1)S(1)}, bf16[8,128,256]{2,1,0:T(8,128)(2,1)}, u32[]{:S(2)}, u32[]{:S(2)}) collective-permute-start(bf16[8,128,256]{2,1,0:T(8,128)(2,1)S(1)} %get-tuple-element.38), channel_id=1, source_target_pairs={{0,16},{16,0},{1,17},{17,1},{2,18},{18,2},{3,19},{19,3},{4,20},{20... | collective-permute-start | bytes 1572872 | tf_op jit(solution)/shard_map/ppermute | solution.py:286
  60.2 1.4 %copy-start.2 = (bf16[16,2,128,256]{3,2,1,0:T(8,128)(2,1)}, bf16[16,2,128,256]{3,2,1,0:T(8,128)(2,1)S(1)}, u32[]{:S(2)}) copy-start(bf16[16,2,128,256]{3,2,1,0:T(8,128)(2,1)S(1)} %all-to-all-done.tokens_ref) | copy-start | bytes 6291460
  61.6 30.9 %all-to-all-start.1 = ((bf16[8,2,128,256]{3,2,1,0:T(8,128)(2,1)}), bf16[8,2,128,256]{3,2,1,0:T(8,128)(2,1)S(1)}, u32[]{:S(2)}, u32[]{:S(2)}) async-start(bf16[8,2,128,256]{3,2,1,0:T(8,128)(2,1)} %pad_maximum_fusion), calls=%async_computation.1 | async-start | bytes 2097152 | tf_op jit(solution)/shard_map/all_to_all | solution.py:291
  66.5 1.6 %copy-start.3 = (bf16[16,2,128,256]{3,2,1,0:T(8,128)(2,1)S(1)}, bf16[16,2,128,256]{3,2,1,0:T(8,128)(2,1)}, u32[]{:S(2)}) copy-start(bf16[16,2,128,256]{3,2,1,0:T(8,128)(2,1)} %copy-done.2) | copy-start | bytes 6291460
  68.1 14.3 %copy-start = (f32[3,1024,256]{2,1,0:T(8,128)S(1)}, f32[3,1024,256]{2,1,0:T(8,128)}, u32[]{:S(2)}) copy-start(f32[3,1024,256]{2,1,0:T(8,128)} %broadcast_select_fusion.1.weight_ref) | copy-start | bytes 9437188
  68.1 14.3 %copy-start.1 = (f32[3,1024,256]{2,1,0:T(8,128)S(1)}, f32[3,1024,256]{2,1,0:T(8,128)}, u32[]{:S(2)}) copy-start(f32[3,1024,256]{2,1,0:T(8,128)} %broadcast_select_fusion.momentum_ref) | copy-start | bytes 9437188
  78.9 3.5 %collective-permute-start.3 = (bf16[3,1024,256]{2,1,0:T(8,128)(2,1)S(1)}, bf16[3,1024,256]{2,1,0:T(8,128)(2,1)S(1)}, u32[]{:S(2)}, u32[]{:S(2)}) collective-permute-start(bf16[3,1024,256]{2,1,0:T(8,128)(2,1)S(1)} %head_gradient.1.refs_0_), channel_id=1, source_target_pairs={{0,8},{8,0},{1,9},{9,1},{2,10},{10,2},{3,11},{11,3},{4,12},{12,4},... | collective-permute-start | bytes 4718600 | tf_op jit(solution)/shard_map/ppermute | solution.py:294
  93.8 8.0 %collective-permute-start.13 = (bf16[1,128,256]{2,1,0:T(8,128)(2,1)S(1)}, bf16[1,128,256]{2,1,0:T(8,128)(2,1)S(1)}, u32[]{:S(2)}, u32[]{:S(2)}) collective-permute-start(bf16[1,128,256]{2,1,0:T(8,128)(2,1)S(1)} %get-tuple-element.34), channel_id=1, source_target_pairs={{0,5},{1,4},{2,7},{3,6},{4,1},{5,0},{6,3},{7,2},{8,13},{9,12},{10,... | collective-permute-start | bytes 196616 | tf_op jit(solution)/shard_map/ppermute | solution.py:310
  94.3 8.5 %collective-permute-start.14 = (bf16[1,128,256]{2,1,0:T(8,128)(2,1)S(1)}, bf16[1,128,256]{2,1,0:T(8,128)(2,1)S(1)}, u32[]{:S(2)}, u32[]{:S(2)}) collective-permute-start(bf16[1,128,256]{2,1,0:T(8,128)(2,1)S(1)} %get-tuple-element.35), channel_id=1, source_target_pairs={{0,6},{1,7},{2,4},{3,5},{4,2},{5,3},{6,0},{7,1},{8,14},{9,15},{10,... | collective-permute-start | bytes 196616 | tf_op jit(solution)/shard_map/ppermute | solution.py:310
  97.9 13.4 %collective-permute-start.5 = (bf16[2,128,256]{2,1,0:T(8,128)(2,1)S(1)}, bf16[2,128,256]{2,1,0:T(8,128)(2,1)S(1)}, u32[]{:S(2)}, u32[]{:S(2)}) collective-permute-start(bf16[2,128,256]{2,1,0:T(8,128)(2,1)S(1)} %get-tuple-element.28), channel_id=1, source_target_pairs={{0,2},{1,3},{2,0},{3,1},{4,6},{5,7},{6,4},{7,5},{8,10},{9,11},{10,... | collective-permute-start | bytes 393224 | tf_op jit(solution)/shard_map/ppermute | solution.py:310
  100.3 11.0 %collective-permute-start.6 = (bf16[2,128,256]{2,1,0:T(8,128)(2,1)S(1)}, bf16[2,128,256]{2,1,0:T(8,128)(2,1)S(1)}, u32[]{:S(2)}, u32[]{:S(2)}) collective-permute-start(bf16[2,128,256]{2,1,0:T(8,128)(2,1)S(1)} %get-tuple-element.29), channel_id=1, source_target_pairs={{0,3},{1,2},{2,1},{3,0},{4,7},{5,6},{6,5},{7,4},{8,11},{9,10},{10,... | collective-permute-start | bytes 393224 | tf_op jit(solution)/shard_map/ppermute | solution.py:310
  101.8 9.5 %collective-permute-start.4 = (bf16[2,128,256]{2,1,0:T(8,128)(2,1)S(1)}, bf16[2,128,256]{2,1,0:T(8,128)(2,1)S(1)}, u32[]{:S(2)}, u32[]{:S(2)}) collective-permute-start(bf16[2,128,256]{2,1,0:T(8,128)(2,1)S(1)} %get-tuple-element.27.after_ref), channel_id=1, source_target_pairs={{0,1},{1,0},{2,3},{3,2},{4,5},{5,4},{6,7},{7,6},{8,9},{9,8},{10,11... | collective-permute-start | bytes 393224 | tf_op jit(solution)/shard_map/ppermute | solution.py:310
  102.8 8.5 %collective-permute-start.15 = (bf16[1,128,256]{2,1,0:T(8,128)(2,1)S(1)}, bf16[1,128,256]{2,1,0:T(8,128)(2,1)S(1)}, u32[]{:S(2)}, u32[]{:S(2)}) collective-permute-start(bf16[1,128,256]{2,1,0:T(8,128)(2,1)S(1)} %get-tuple-element.36), channel_id=1, source_target_pairs={{0,7},{1,6},{2,5},{3,4},{4,3},{5,2},{6,1},{7,0},{8,15},{9,14},{10,... | collective-permute-start | bytes 196616 | tf_op jit(solution)/shard_map/ppermute | solution.py:310
  105.1 6.2 %collective-permute-start.12 = (bf16[1,128,256]{2,1,0:T(8,128)(2,1)S(1)}, bf16[1,128,256]{2,1,0:T(8,128)(2,1)S(1)}, u32[]{:S(2)}, u32[]{:S(2)}) collective-permute-start(bf16[1,128,256]{2,1,0:T(8,128)(2,1)S(1)} %get-tuple-element.25.refs_0_), channel_id=1, source_target_pairs={{0,4},{1,5},{2,6},{3,7},{4,0},{5,1},{6,2},{7,3},{8,12},{9,13},{10,... | collective-permute-start | bytes 196616 | tf_op jit(solution)/shard_map/ppermute | solution.py:310
  113.1 24.7 %collective-permute-start.16 = (bf16[128,3072]{1,0:T(8,128)(2,1)S(1)}, bf16[128,3072]{1,0:T(8,128)(2,1)S(1)}, u32[]{:S(2)}, u32[]{:S(2)}) collective-permute-start(bf16[128,3072]{1,0:T(8,128)(2,1)S(1)} %project.3.after_ref), channel_id=1, source_target_pairs={{0,16},{16,0},{1,17},{17,1},{2,18},{18,2},{3,19},{19,3},{4,20},{20... | collective-permute-start | bytes 2359304 | tf_op jit(solution)/shard_map/ppermute | solution.py:332
  117.4 20.4 %collective-permute-start.17 = (bf16[128,1024]{1,0:T(8,128)(2,1)S(1)}, bf16[128,1024]{1,0:T(8,128)(2,1)S(1)}, u32[]{:S(2)}, u32[]{:S(2)}) collective-permute-start(bf16[128,1024]{1,0:T(8,128)(2,1)S(1)} %project.5), channel_id=1, source_target_pairs={{0,16},{16,0},{1,17},{17,1},{2,18},{18,2},{3,19},{19,3},{4,20},{20... | collective-permute-start | bytes 786440 | tf_op jit(solution)/shard_map/ppermute | solution.py:336
  118.3 9.9 %collective-permute-start.9 = (bf16[1,128,256]{2,1,0:T(8,128)(2,1)S(1)}, bf16[1,128,256]{2,1,0:T(8,128)(2,1)S(1)}, u32[]{:S(2)}, u32[]{:S(2)}) collective-permute-start(bf16[1,128,256]{2,1,0:T(8,128)(2,1)S(1)} %get-tuple-element.31), channel_id=1, source_target_pairs={{0,5},{1,4},{2,7},{3,6},{4,1},{5,0},{6,3},{7,2},{8,13},{9,12},{10,... | collective-permute-start | bytes 196616 | tf_op jit(solution)/shard_map/ppermute | solution.py:310
  121.5 6.7 %collective-permute-start.10 = (bf16[1,128,256]{2,1,0:T(8,128)(2,1)S(1)}, bf16[1,128,256]{2,1,0:T(8,128)(2,1)S(1)}, u32[]{:S(2)}, u32[]{:S(2)}) collective-permute-start(bf16[1,128,256]{2,1,0:T(8,128)(2,1)S(1)} %get-tuple-element.32), channel_id=1, source_target_pairs={{0,6},{1,7},{2,4},{3,5},{4,2},{5,3},{6,0},{7,1},{8,14},{9,15},{10,... | collective-permute-start | bytes 196616 | tf_op jit(solution)/shard_map/ppermute | solution.py:310
  123.4 7.1 %collective-permute-start.11 = (bf16[1,128,256]{2,1,0:T(8,128)(2,1)S(1)}, bf16[1,128,256]{2,1,0:T(8,128)(2,1)S(1)}, u32[]{:S(2)}, u32[]{:S(2)}) collective-permute-start(bf16[1,128,256]{2,1,0:T(8,128)(2,1)S(1)} %get-tuple-element.33), channel_id=1, source_target_pairs={{0,7},{1,6},{2,5},{3,4},{4,3},{5,2},{6,1},{7,0},{8,15},{9,14},{10,... | collective-permute-start | bytes 196616 | tf_op jit(solution)/shard_map/ppermute | solution.py:310
  128.2 5.2 %collective-permute-start.8 = (bf16[1,128,256]{2,1,0:T(8,128)(2,1)S(1)}, bf16[1,128,256]{2,1,0:T(8,128)(2,1)S(1)}, u32[]{:S(2)}, u32[]{:S(2)}) collective-permute-start(bf16[1,128,256]{2,1,0:T(8,128)(2,1)S(1)} %get-tuple-element.30.refs_9_), channel_id=1, source_target_pairs={{0,4},{1,5},{2,6},{3,7},{4,0},{5,1},{6,2},{7,3},{8,12},{9,13},{10,... | collective-permute-start | bytes 196616 | tf_op jit(solution)/shard_map/ppermute | solution.py:310
  (1 other events, 1.4 us)

commit v4 on v3

--- a/solution.py
+++ b/solution.py
@@ -38,7 +38,7 @@
 def pack(key_rows, value_rows, token_rates, width, scale):
     rows, columns = key_rows.shape
     heads = columns // width
-    group = 4 if heads % 4 == 0 else 1
+    group = 8 if heads % 8 == 0 else 1
     return pl.pallas_call(
         functools.partial(pack_kernel, scale, group),
         grid=(heads // group,),
@@ -48,7 +48,7 @@
             pl.BlockSpec(token_rates.shape[::-1], lambda h: (0, 0)),
         ],
         out_specs=pl.BlockSpec((group, 2, rows, width), lambda h: (h, 0, 0, 0)),
-        out_shape=jax.ShapeDtypeStruct((heads, 2, rows, width), key_rows.dtype),
+        out_shape=pltpu.HBM((heads, 2, rows, width), key_rows.dtype),
         compiler_params=pltpu.CompilerParams(vmem_limit_bytes=VMEM),
         name="pack",
     )(
@@ -260,6 +260,73 @@
         cost_estimate=SMALL,
         name="project",
     )(*mixed, *weights, *after)
+
+
+def finish_kernel(places, pieces, *refs):
+    terms = len(places)
+    mixed_refs, weight_refs = refs[:terms], refs[terms : terms + pieces]
+    received_refs = refs[terms + pieces : -3]
+    out_ref, rest_ref, depth_ref = refs[-3:]
+    head = lax.axis_index("hd")
+    for i, (ref, place) in enumerate(zip(mixed_refs, places)):
+        depth_ref[jnp.bitwise_xor(head, i)] = ref[place]
+    mixed = jnp.concatenate([depth_ref[i] for i in range(terms)], axis=1)
+    for weight_ref in weight_refs:
+        columns = weight_ref.shape[1]
+        block = 512 if columns % 512 == 0 else columns
+        for start in range(0, columns, block):
+            part = f32_dot(mixed, weight_ref[:, start : start + block])
+            if weight_ref is weight_refs[0]:
+                for ref in received_refs:
+                    part = part + ref[:, start : start + block].astype(jnp.float32)
+                out_ref[:, start : start + block] = part.astype(out_ref.dtype)
+            else:
+                rest_ref[:, start : start + block] = part
+
+
+def finish(blocks, weights, received):
+    mixed, places = zip(*blocks)
+    _, rows, width = mixed[0].shape
+    whole = pl.BlockSpec(memory_space=pltpu.VMEM)
+    first, last = (w.shape[1] for w in weights)
+    weights = [pltpu.with_memory_space_constraint(w, pltpu.VMEM) for w in weights]
+    return pl.pallas_call(
+        functools.partial(finish_kernel, places, len(weights)),
+        in_specs=[whole] * (len(mixed) + len(weights) + len(received)),
+        out_specs=[whole] * 2,
+        out_shape=[
+            jax.ShapeDtypeStruct((rows, first + last), jnp.bfloat16),
+            jax.ShapeDtypeStruct((rows, last), jnp.float32),
+        ],
+        scratch_shapes=[pltpu.VMEM((len(mixed), rows, width), mixed[0].dtype)],
+        compiler_params=pltpu.CompilerParams(vmem_limit_bytes=VMEM),
+        cost_estimate=SMALL,
+        name="finish",
+    )(*mixed, *weights, *received)
+
+
+def close_kernel(whole_ref, rest_ref, *refs):
+    total = rest_ref[...]
+    for ref in refs[:-1]:
+        total = total + ref[...].astype(jnp.float32)
+    refs[-1][...] = total.astype(refs[-1].dtype)
+
+
+def close(result, rest, received):
+    rows, columns = rest.shape
+    place = result.shape[1] // columns - 1
+    block = pl.BlockSpec((rows, columns), lambda n: (0, 0))
+    return pl.pallas_call(
+        close_kernel,
+        grid=(1,),
+        in_specs=[pl.BlockSpec(memory_space=pl.ANY)] + [block] * (1 + len(received)),
+        out_specs=pl.BlockSpec((rows, columns), lambda n: (0, place)),
+        out_shape=jax.ShapeDtypeStruct(result.shape, result.dtype),
+        input_output_aliases={0: 0},
+        compiler_params=pltpu.CompilerParams(vmem_limit_bytes=VMEM),
+        cost_estimate=SMALL,
+        name="close",
+    )(result, rest, *received)
 
 
 def shards(query_rows, key_rows, value_rows, token_rates, fast_weights, momentum, out_weight):
@@ -335,9 +402,8 @@
             done = project(blocks, held[1:], jnp.bfloat16, [])
             received[1].append(lax.ppermute(done, "x", over))
         else:
-            own = project(blocks, held, jnp.float32, [])
-    sums = [functools.reduce(jnp.add, [p.astype(jnp.float32) for p in r]) for r in received]
-    return (own + jnp.concatenate(sums, axis=1)).astype(jnp.bfloat16)
+            result, rest = finish(blocks, held, received[0])
+    return close(result, rest, received[1])
 
 
 def solution(mesh):

time: 140 us -> 138 us (0.986)
  Pallas kernels: 34.4 us -> 35.9 us
    pallas_call x0 -> x2, Pallas kernels: none -> 3.92 us  [the longest x1 3.17 us: finish(): pl.pallas_call(functools.partial(finish_kernel, places, len(weights)), in...]
    pallas_call x3 -> x2, Pallas kernels: 4.9 us -> 2.56 us  [project(): pl.pallas_call(functools.partial(project_kernel, places, len(weights)), i...]
    unnamed x10 -> x8, local copies, waits for them, and re-layouts: 4.36 us -> 3.01 us
  transfers between devices with their start and end apart: 20 -> 20, of which waited for: 9 -> 10; matrix products, arithmetic and copies ran while one was open for 13% -> 13% of each run, Pallas kernels for 23% -> 24%
where the time goes in v4:
time: 138 us; the launch traced here: 137 us
  waiting for transfers between devices  46.6 us (34%)
  Pallas kernels  35.9 us (26%)
  starting transfers between devices  34 us (25%)
  local copies, waits for them, and re-layouts  10.6 us (8%)
  other arithmetic  9.99 us (7%)
    ppermute x1, waiting for transfers between devices, shards(): lax.ppermute(turned[d], 'x', [(i, (i - d) % sides) for i in range(sides)])  19.8 us
    ppermute x11, starting transfers between devices, spread(): lax.ppermute(block, 'hd', partner[i])  16 us
    pallas_call x1, Pallas kernels, head_gradient(): pl.pallas_call(functools.partial(gradient_kernel, max(1, min(sources, 512...  10.8 us
    ppermute x11, waiting for transfers between devices, spread(): lax.ppermute(block, 'hd', partner[i])  8.61 us
    all_to_all x1, starting transfers between devices, shards(): tokens = lax.all_to_all(payload, ('x', 'hd'), 0, 0, tiled=True)  7.87 us
    all_to_all x1, waiting for transfers between devices, shards(): queries = lax.all_to_all(ready, 'hd', 0, 0, tiled=True)  7.06 us
    pallas_call x2, Pallas kernels, hold(): pl.pallas_call(functools.partial(hold_kernel, start), in_specs=[pl.BlockS...  6.87 us
    all_to_all x1, waiting for transfers between devices, shards(): tokens = lax.all_to_all(payload, ('x', 'hd'), 0, 0, tiled=True)  6.45 us
  transfers between devices with their start and end apart: 20, of which 10 were waited for; matrix products, arithmetic and copies ran while one was open for 13% of the time, Pallas kernels for 24%

profile of v4, /device:TPU:0, one launch (start us, length us, event | category | flops | bytes accessed | tf_op | source)
XLA Modules:
  0.0 137.2 jit_solution(15840309614723436110)
XLA Ops:
  0.5 2.9 %pack.1 = bf16[16,2,128,256]{3,2,1,0:T(8,128)(2,1)} custom-call(bf16[128,4096]{1,0:T(8,128)(2,1)} %key_ref.1, bf16[128,4096]{1,0:T(8,128)(2,1)} %value_ref.1, f32[16,128]{1,0:T(8,128)} %bitcast.15), custom_call_target="tpu_custom_call" | custom-call | tf_op jit(solution)/shard_map/pack/pallas_call | solution.py:42
  3.3 7.9 %all-to-all-start = ((bf16[16,2,128,256]{3,2,1,0:T(8,128)(2,1)}), bf16[16,2,128,256]{3,2,1,0:T(8,128)(2,1)S(1)}, u32[]{:S(2)}, u32[]{:S(2)}) async-start(bf16[16,2,128,256]{3,2,1,0:T(8,128)(2,1)} %pack.1), calls=%async_computation | async-start | bytes 4194304 | tf_op jit(solution)/shard_map/all_to_all | solution.py:342
  11.2 3.7 %dynamic-slice_bitcast_fusion = f32[3,1024,256]{2,1,0:T(8,128)} fusion(f32[4,3,1024,256]{3,2,1,0:T(8,128)} %param.12, s32[]{:T(128)S(6)} %select_n.33), kind=kLoop, calls=%fused_computation | loop fusion | bytes 6291460 | tf_op jit(solution)/shard_map/jit(dynamic_index_in_dim)/squeeze | solution.py:346
  15.2 3.7 %dynamic-slice_bitcast_fusion.1 = f32[3,1024,256]{2,1,0:T(8,128)} fusion(f32[4,3,1024,256]{3,2,1,0:T(8,128)} %param.11, s32[]{:T(128)S(6)} %select_n.33), kind=kLoop, calls=%fused_computation.1 | loop fusion | bytes 6291460 | tf_op jit(solution)/shard_map/jit(dynamic_index_in_dim)/squeeze | solution.py:345
  22.5 19.8 %collective-permute-done = bf16[8,128,256]{2,1,0:T(8,128)(2,1)} collective-permute-done((bf16[8,128,256]{2,1,0:T(8,128)(2,1)S(1)}, bf16[8,128,256]{2,1,0:T(8,128)(2,1)}, u32[]{:S(2)}, u32[]{:S(2)}) %collective-permute-start) | collective-permute-done | bytes 524320 | tf_op jit(solution)/shard_map/ppermute | solution.py:353
  42.3 2.1 %pad_maximum_fusion = bf16[8,2,128,256]{3,2,1,0:T(8,128)(2,1)} fusion(bf16[8,1,128,256]{3,2,1,0:T(8,128)(2,1)} %bitcast.3, bf16[8,1,128,256]{3,2,1,0:T(8,128)(2,1)S(1)} %get-tuple-element.41), kind=kLoop, calls=%fused_computation.4 | loop fusion | flops 524288 | bytes 2097152 | tf_op jit(solution)/shard_map/stack | solution.py:356
  44.4 3.9 %broadcast_select_fusion.momentum_ref = f32[3,1024,256]{2,1,0:T(8,128)} fusion(f32[3,1024,256]{2,1,0:T(8,128)} %collective-permute-done.2, pred[]{:T(512)S(6)} %eq.6, f32[4,3,1024,256]{3,2,1,0:T(8,128)} %param.12, s32[]{:T(128)S(6)} %select_n.33), kind=kLoop, calls=%fused_computation.2 | loop fusion | flops 786432 | bytes 9437189 | tf_op jit(solution)/shard_map/jit(_where)/select_n | solution.py:348
  48.4 3.9 %broadcast_select_fusion.1.weight_ref = f32[3,1024,256]{2,1,0:T(8,128)} fusion(f32[3,1024,256]{2,1,0:T(8,128)} %collective-permute-done.1, pred[]{:T(512)S(6)} %eq.6, f32[4,3,1024,256]{3,2,1,0:T(8,128)} %param.11, s32[]{:T(128)S(6)} %select_n.33), kind=kLoop, calls=%fused_computation.3 | loop fusion | flops 786432 | bytes 9437189 | tf_op jit(solution)/shard_map/jit(_where)/select_n | solution.py:347
  52.3 6.4 %all-to-all-done.tokens_ref = bf16[16,2,128,256]{3,2,1,0:T(8,128)(2,1)S(1)} async-done(((bf16[16,2,128,256]{3,2,1,0:T(8,128)(2,1)}), bf16[16,2,128,256]{3,2,1,0:T(8,128)(2,1)S(1)}, u32[]{:S(2)}, u32[]{:S(2)}) %all-to-all-start) | async-done | bytes 2097184 | tf_op jit(solution)/shard_map/all_to_all | solution.py:342
  60.2 4.9 %all-to-all-start.1 = ((bf16[8,2,128,256]{3,2,1,0:T(8,128)(2,1)}), bf16[8,2,128,256]{3,2,1,0:T(8,128)(2,1)S(1)}, u32[]{:S(2)}, u32[]{:S(2)}) async-start(bf16[8,2,128,256]{3,2,1,0:T(8,128)(2,1)} %pad_maximum_fusion), calls=%async_computation.1 | async-start | bytes 2097152 | tf_op jit(solution)/shard_map/all_to_all | solution.py:358
  66.7 10.8 %head_gradient.1.refs_0_ = bf16[3,1024,256]{2,1,0:T(8,128)(2,1)S(1)} custom-call(bf16[16,2,128,256]{3,2,1,0:T(8,128)(2,1)S(1)} %copy-done.3, f32[3,1024,256]{2,1,0:T(8,128)} %broadcast_select_fusion.1.weight_ref), custom_call_target="tpu_custom_call" | custom-call | flops 1024 | bytes 1024 | tf_op jit(solution)/shard_map/head_gradient/pallas_call | solution.py:144
  77.6 3.4 %collective-permute-done.3.refs_1_ = bf16[3,1024,256]{2,1,0:T(8,128)(2,1)S(1)} collective-permute-done((bf16[3,1024,256]{2,1,0:T(8,128)(2,1)S(1)}, bf16[3,1024,256]{2,1,0:T(8,128)(2,1)S(1)}, u32[]{:S(2)}, u32[]{:S(2)}) %collective-permute-start.3) | collective-permute-done | bytes 1572896 | tf_op jit(solution)/shard_map/ppermute | solution.py:361
  81.0 3.0 %update.1.normed_ref = bf16[3,1024,256]{2,1,0:T(8,128)(2,1)S(1)} custom-call(f32[3,1024,256]{2,1,0:T(8,128)S(1)} %copy-done, f32[3,1024,256]{2,1,0:T(8,128)S(1)} %copy-done.1, bf16[3,1024,256]{2,1,0:T(8,128)(2,1)S(1)} %head_gradient.1.refs_0_, bf16[3,1024,256]{2,1,0:T(8,128)(2,1)S(1)} %collective-permute-done.3.refs_1_), custom_call_target="tpu_custom_call" | custom-call | flops 1024 | bytes 1024 | tf_op jit(solution)/shard_map/update/pallas_call | solution.py:184
  84.0 7.1 %all-to-all-done.1.query_ref = bf16[8,2,128,256]{3,2,1,0:T(8,128)(2,1)S(1)} async-done(((bf16[8,2,128,256]{3,2,1,0:T(8,128)(2,1)}), bf16[8,2,128,256]{3,2,1,0:T(8,128)(2,1)S(1)}, u32[]{:S(2)}, u32[]{:S(2)}) %all-to-all-start.1) | async-done | bytes 1048608 | tf_op jit(solution)/shard_map/all_to_all | solution.py:358
  96.5 2.4 %collective-permute-start.5 = (bf16[2,128,256]{2,1,0:T(8,128)(2,1)S(1)}, bf16[2,128,256]{2,1,0:T(8,128)(2,1)S(1)}, u32[]{:S(2)}, u32[]{:S(2)}) collective-permute-start(bf16[2,128,256]{2,1,0:T(8,128)(2,1)S(1)} %get-tuple-element.30), channel_id=1, source_target_pairs={{0,2},{1,3},{2,0},{3,1},{4,6},{5,7},{6,4},{7,5},{8,10},{9,11},{10,... | collective-permute-start | bytes 393224 | tf_op jit(solution)/shard_map/ppermute | solution.py:377
  101.4 2.3 %collective-permute-start.15 = (bf16[1,128,256]{2,1,0:T(8,128)(2,1)S(1)}, bf16[1,128,256]{2,1,0:T(8,128)(2,1)S(1)}, u32[]{:S(2)}, u32[]{:S(2)}) collective-permute-start(bf16[1,128,256]{2,1,0:T(8,128)(2,1)S(1)} %get-tuple-element.38), channel_id=1, source_target_pairs={{0,7},{1,6},{2,5},{3,4},{4,3},{5,2},{6,1},{7,0},{8,15},{9,14},{10,... | collective-permute-start | bytes 196616 | tf_op jit(solution)/shard_map/ppermute | solution.py:377
  103.9 4.6 %hold.2.refs_0_.refs_8_ = bf16[2048,3072]{1,0:T(8,128)(2,1)S(1)} custom-call(bf16[1024,4096]{1,0:T(8,128)(2,1)} %own_ref.3, bf16[1024,4096]{1,0:T(8,128)(2,1)} %collective-permute-done.7.other_ref, bf16[2,128,256]{2,1,0:T(8,128)(2,1)S(1)} %get-tuple-element.29.after_ref), custom_call_target="tpu_custom_call" | custom-call | flops 1024 | bytes 1024 | tf_op jit(solution)/shard_map/hold/pallas_call | solution.py:107
  113.1 2.2 %hold.3.refs_9_.refs_8_ = bf16[2048,1024]{1,0:T(8,128)(2,1)S(1)} custom-call(bf16[1024,4096]{1,0:T(8,128)(2,1)} %own_ref.3, bf16[1024,4096]{1,0:T(8,128)(2,1)} %collective-permute-done.7.other_ref, bf16[128,3072]{1,0:T(8,128)(2,1)S(1)} %project.2.after_ref), custom_call_target="tpu_custom_call" | custom-call | flops 1024 | bytes 1024 | tf_op jit(solution)/shard_map/hold/pallas_call | solution.py:107
  116.9 3.3 %collective-permute-start.9 = (bf16[1,128,256]{2,1,0:T(8,128)(2,1)S(1)}, bf16[1,128,256]{2,1,0:T(8,128)(2,1)S(1)}, u32[]{:S(2)}, u32[]{:S(2)}) collective-permute-start(bf16[1,128,256]{2,1,0:T(8,128)(2,1)S(1)} %get-tuple-element.33), channel_id=1, source_target_pairs={{0,5},{1,4},{2,7},{3,6},{4,1},{5,0},{6,3},{7,2},{8,13},{9,12},{10,... | collective-permute-start | bytes 196616 | tf_op jit(solution)/shard_map/ppermute | solution.py:377
  122.0 2.3 %collective-permute-start.11 = (bf16[1,128,256]{2,1,0:T(8,128)(2,1)S(1)}, bf16[1,128,256]{2,1,0:T(8,128)(2,1)S(1)}, u32[]{:S(2)}, u32[]{:S(2)}) collective-permute-start(bf16[1,128,256]{2,1,0:T(8,128)(2,1)S(1)} %get-tuple-element.35), channel_id=1, source_target_pairs={{0,7},{1,6},{2,5},{3,4},{4,3},{5,2},{6,1},{7,0},{8,15},{9,14},{10,... | collective-permute-start | bytes 196616 | tf_op jit(solution)/shard_map/ppermute | solution.py:377
  124.3 2.5 %collective-permute-done.9.refs_5_ = bf16[1,128,256]{2,1,0:T(8,128)(2,1)S(1)} collective-permute-done((bf16[1,128,256]{2,1,0:T(8,128)(2,1)S(1)}, bf16[1,128,256]{2,1,0:T(8,128)(2,1)S(1)}, u32[]{:S(2)}, u32[]{:S(2)}) %collective-permute-start.9) | collective-permute-done | bytes 65568 | tf_op jit(solution)/shard_map/ppermute | solution.py:377
  126.8 2.2 %collective-permute-done.11.refs_7_ = bf16[1,128,256]{2,1,0:T(8,128)(2,1)S(1)} collective-permute-done((bf16[1,128,256]{2,1,0:T(8,128)(2,1)S(1)}, bf16[1,128,256]{2,1,0:T(8,128)(2,1)S(1)}, u32[]{:S(2)}, u32[]{:S(2)}) %collective-permute-start.11) | collective-permute-done | bytes 65568 | tf_op jit(solution)/shard_map/ppermute | solution.py:377
  129.0 2.9 %collective-permute-done.8.refs_4_ = bf16[1,128,256]{2,1,0:T(8,128)(2,1)S(1)} collective-permute-done((bf16[1,128,256]{2,1,0:T(8,128)(2,1)S(1)}, bf16[1,128,256]{2,1,0:T(8,128)(2,1)S(1)}, u32[]{:S(2)}, u32[]{:S(2)}) %collective-permute-start.8) | collective-permute-done | bytes 65568 | tf_op jit(solution)/shard_map/ppermute | solution.py:377
  132.3 3.2 %finish.1 = (bf16[128,4096]{1,0:T(8,128)(2,1)}, f32[128,1024]{1,0:T(8,128)S(1)}) custom-call(bf16[2,128,256]{2,1,0:T(8,128)(2,1)S(1)} %get-tuple-element.28.refs_0_, bf16[2,128,256]{2,1,0:T(8,128)(2,1)S(1)} %collective-permute-done.4.refs_1_, bf16[2,128,256]{2,1,0:T(8,128)(2,1)S(1)} %collective-permute-done.5.refs_2_, ...), custom_call_target="tpu_custom_call" | custom-call | flops 1024 | bytes 1024 | tf_op jit(solution)/shard_map/finish/pallas_call | solution.py:293
  (43 shorter events, 25.3 us)
Async XLA Ops:
  0.0 103.7 %collective-permute-start.7 = (bf16[1024,4096]{1,0:T(8,128)(2,1)}, bf16[1024,4096]{1,0:T(8,128)(2,1)}, u32[]{:S(2)}, u32[]{:S(2)}) collective-permute-start(bf16[1024,4096]{1,0:T(8,128)(2,1)} %own_ref.3), channel_id=1, source_target_pairs={{0,8},{8,0},{1,9},{9,1},{2,10},{10,2},{3,11},{11,3},{4,12},{12,4},... | collective-permute-start | bytes 25165832 | tf_op jit(solution)/shard_map/ppermute | solution.py:349
  3.3 55.4 %all-to-all-start = ((bf16[16,2,128,256]{3,2,1,0:T(8,128)(2,1)}), bf16[16,2,128,256]{3,2,1,0:T(8,128)(2,1)S(1)}, u32[]{:S(2)}, u32[]{:S(2)}) async-start(bf16[16,2,128,256]{3,2,1,0:T(8,128)(2,1)} %pack.1), calls=%async_computation | async-start | bytes 4194304 | tf_op jit(solution)/shard_map/all_to_all | solution.py:342
  15.0 29.5 %collective-permute-start.2 = (f32[3,1024,256]{2,1,0:T(8,128)}, f32[3,1024,256]{2,1,0:T(8,128)}, u32[]{:S(2)}, u32[]{:S(2)}) collective-permute-start(f32[3,1024,256]{2,1,0:T(8,128)} %dynamic-slice_bitcast_fusion), channel_id=1, source_target_pairs={{0,8},{8,0},{1,9},{9,1},{2,10},{10,2},{3,11},{11,3},{4,12},{12,4},... | collective-permute-start | bytes 9437192 | tf_op jit(solution)/shard_map/ppermute | solution.py:348
  18.9 29.5 %collective-permute-start.1 = (f32[3,1024,256]{2,1,0:T(8,128)}, f32[3,1024,256]{2,1,0:T(8,128)}, u32[]{:S(2)}, u32[]{:S(2)}) collective-permute-start(f32[3,1024,256]{2,1,0:T(8,128)} %dynamic-slice_bitcast_fusion.1), channel_id=1, source_target_pairs={{0,8},{8,0},{1,9},{9,1},{2,10},{10,2},{3,11},{11,3},{4,12},{12,4},... | collective-permute-start | bytes 9437192 | tf_op jit(solution)/shard_map/ppermute | solution.py:347
  20.6 21.8 %collective-permute-start = (bf16[8,128,256]{2,1,0:T(8,128)(2,1)S(1)}, bf16[8,128,256]{2,1,0:T(8,128)(2,1)}, u32[]{:S(2)}, u32[]{:S(2)}) collective-permute-start(bf16[8,128,256]{2,1,0:T(8,128)(2,1)S(1)} %get-tuple-element.42), channel_id=1, source_target_pairs={{0,16},{16,0},{1,17},{17,1},{2,18},{18,2},{3,19},{19,3},{4,20},{20... | collective-permute-start | bytes 1572872 | tf_op jit(solution)/shard_map/ppermute | solution.py:353
  58.8 1.4 %copy-start.2 = (bf16[16,2,128,256]{3,2,1,0:T(8,128)(2,1)}, bf16[16,2,128,256]{3,2,1,0:T(8,128)(2,1)S(1)}, u32[]{:S(2)}) copy-start(bf16[16,2,128,256]{3,2,1,0:T(8,128)(2,1)S(1)} %all-to-all-done.tokens_ref) | copy-start | bytes 6291460
  60.2 30.9 %all-to-all-start.1 = ((bf16[8,2,128,256]{3,2,1,0:T(8,128)(2,1)}), bf16[8,2,128,256]{3,2,1,0:T(8,128)(2,1)S(1)}, u32[]{:S(2)}, u32[]{:S(2)}) async-start(bf16[8,2,128,256]{3,2,1,0:T(8,128)(2,1)} %pad_maximum_fusion), calls=%async_computation.1 | async-start | bytes 2097152 | tf_op jit(solution)/shard_map/all_to_all | solution.py:358
  65.1 1.6 %copy-start.3 = (bf16[16,2,128,256]{3,2,1,0:T(8,128)(2,1)S(1)}, bf16[16,2,128,256]{3,2,1,0:T(8,128)(2,1)}, u32[]{:S(2)}) copy-start(bf16[16,2,128,256]{3,2,1,0:T(8,128)(2,1)} %copy-done.2) | copy-start | bytes 6291460
  66.7 14.3 %copy-start = (f32[3,1024,256]{2,1,0:T(8,128)S(1)}, f32[3,1024,256]{2,1,0:T(8,128)}, u32[]{:S(2)}) copy-start(f32[3,1024,256]{2,1,0:T(8,128)} %broadcast_select_fusion.1.weight_ref) | copy-start | bytes 9437188
  66.7 14.3 %copy-start.1 = (f32[3,1024,256]{2,1,0:T(8,128)S(1)}, f32[3,1024,256]{2,1,0:T(8,128)}, u32[]{:S(2)}) copy-start(f32[3,1024,256]{2,1,0:T(8,128)} %broadcast_select_fusion.momentum_ref) | copy-start | bytes 9437188
  77.5 3.5 %collective-permute-start.3 = (bf16[3,1024,256]{2,1,0:T(8,128)(2,1)S(1)}, bf16[3,1024,256]{2,1,0:T(8,128)(2,1)S(1)}, u32[]{:S(2)}, u32[]{:S(2)}) collective-permute-start(bf16[3,1024,256]{2,1,0:T(8,128)(2,1)S(1)} %head_gradient.1.refs_0_), channel_id=1, source_target_pairs={{0,8},{8,0},{1,9},{9,1},{2,10},{10,2},{3,11},{11,3},{4,12},{12,4},... | collective-permute-start | bytes 4718600 | tf_op jit(solution)/shard_map/ppermute | solution.py:361
  92.4 8.0 %collective-permute-start.13 = (bf16[1,128,256]{2,1,0:T(8,128)(2,1)S(1)}, bf16[1,128,256]{2,1,0:T(8,128)(2,1)S(1)}, u32[]{:S(2)}, u32[]{:S(2)}) collective-permute-start(bf16[1,128,256]{2,1,0:T(8,128)(2,1)S(1)} %get-tuple-element.36), channel_id=1, source_target_pairs={{0,5},{1,4},{2,7},{3,6},{4,1},{5,0},{6,3},{7,2},{8,13},{9,12},{10,... | collective-permute-start | bytes 196616 | tf_op jit(solution)/shard_map/ppermute | solution.py:377
  92.9 8.4 %collective-permute-start.14 = (bf16[1,128,256]{2,1,0:T(8,128)(2,1)S(1)}, bf16[1,128,256]{2,1,0:T(8,128)(2,1)S(1)}, u32[]{:S(2)}, u32[]{:S(2)}) collective-permute-start(bf16[1,128,256]{2,1,0:T(8,128)(2,1)S(1)} %get-tuple-element.37), channel_id=1, source_target_pairs={{0,6},{1,7},{2,4},{3,5},{4,2},{5,3},{6,0},{7,1},{8,14},{9,15},{10,... | collective-permute-start | bytes 196616 | tf_op jit(solution)/shard_map/ppermute | solution.py:377
  96.5 13.4 %collective-permute-start.5 = (bf16[2,128,256]{2,1,0:T(8,128)(2,1)S(1)}, bf16[2,128,256]{2,1,0:T(8,128)(2,1)S(1)}, u32[]{:S(2)}, u32[]{:S(2)}) collective-permute-start(bf16[2,128,256]{2,1,0:T(8,128)(2,1)S(1)} %get-tuple-element.30), channel_id=1, source_target_pairs={{0,2},{1,3},{2,0},{3,1},{4,6},{5,7},{6,4},{7,5},{8,10},{9,11},{10,... | collective-permute-start | bytes 393224 | tf_op jit(solution)/shard_map/ppermute | solution.py:377
  98.9 11.0 %collective-permute-start.6 = (bf16[2,128,256]{2,1,0:T(8,128)(2,1)S(1)}, bf16[2,128,256]{2,1,0:T(8,128)(2,1)S(1)}, u32[]{:S(2)}, u32[]{:S(2)}) collective-permute-start(bf16[2,128,256]{2,1,0:T(8,128)(2,1)S(1)} %get-tuple-element.31), channel_id=1, source_target_pairs={{0,3},{1,2},{2,1},{3,0},{4,7},{5,6},{6,5},{7,4},{8,11},{9,10},{10,... | collective-permute-start | bytes 393224 | tf_op jit(solution)/shard_map/ppermute | solution.py:377
  100.4 9.5 %collective-permute-start.4 = (bf16[2,128,256]{2,1,0:T(8,128)(2,1)S(1)}, bf16[2,128,256]{2,1,0:T(8,128)(2,1)S(1)}, u32[]{:S(2)}, u32[]{:S(2)}) collective-permute-start(bf16[2,128,256]{2,1,0:T(8,128)(2,1)S(1)} %get-tuple-element.29.after_ref), channel_id=1, source_target_pairs={{0,1},{1,0},{2,3},{3,2},{4,5},{5,4},{6,7},{7,6},{8,9},{9,8},{10,11... | collective-permute-start | bytes 393224 | tf_op jit(solution)/shard_map/ppermute | solution.py:377
  101.4 8.5 %collective-permute-start.15 = (bf16[1,128,256]{2,1,0:T(8,128)(2,1)S(1)}, bf16[1,128,256]{2,1,0:T(8,128)(2,1)S(1)}, u32[]{:S(2)}, u32[]{:S(2)}) collective-permute-start(bf16[1,128,256]{2,1,0:T(8,128)(2,1)S(1)} %get-tuple-element.38), channel_id=1, source_target_pairs={{0,7},{1,6},{2,5},{3,4},{4,3},{5,2},{6,1},{7,0},{8,15},{9,14},{10,... | collective-permute-start | bytes 196616 | tf_op jit(solution)/shard_map/ppermute | solution.py:377
  103.7 6.2 %collective-permute-start.12 = (bf16[1,128,256]{2,1,0:T(8,128)(2,1)S(1)}, bf16[1,128,256]{2,1,0:T(8,128)(2,1)S(1)}, u32[]{:S(2)}, u32[]{:S(2)}) collective-permute-start(bf16[1,128,256]{2,1,0:T(8,128)(2,1)S(1)} %get-tuple-element.27.refs_0_), channel_id=1, source_target_pairs={{0,4},{1,5},{2,6},{3,7},{4,0},{5,1},{6,2},{7,3},{8,12},{9,13},{10,... | collective-permute-start | bytes 196616 | tf_op jit(solution)/shard_map/ppermute | solution.py:377
  111.7 20.5 %collective-permute-start.16 = (bf16[128,3072]{1,0:T(8,128)(2,1)S(1)}, bf16[128,3072]{1,0:T(8,128)(2,1)S(1)}, u32[]{:S(2)}, u32[]{:S(2)}) collective-permute-start(bf16[128,3072]{1,0:T(8,128)(2,1)S(1)} %project.2.after_ref), channel_id=1, source_target_pairs={{0,16},{16,0},{1,17},{17,1},{2,18},{18,2},{3,19},{19,3},{4,20},{20... | collective-permute-start | bytes 2359304 | tf_op jit(solution)/shard_map/ppermute | solution.py:399
  116.0 20.4 %collective-permute-start.17 = (bf16[128,1024]{1,0:T(8,128)(2,1)S(1)}, bf16[128,1024]{1,0:T(8,128)(2,1)S(1)}, u32[]{:S(2)}, u32[]{:S(2)}) collective-permute-start(bf16[128,1024]{1,0:T(8,128)(2,1)S(1)} %project.3), channel_id=1, source_target_pairs={{0,16},{16,0},{1,17},{17,1},{2,18},{18,2},{3,19},{19,3},{4,20},{20... | collective-permute-start | bytes 786440 | tf_op jit(solution)/shard_map/ppermute | solution.py:403
  116.9 9.9 %collective-permute-start.9 = (bf16[1,128,256]{2,1,0:T(8,128)(2,1)S(1)}, bf16[1,128,256]{2,1,0:T(8,128)(2,1)S(1)}, u32[]{:S(2)}, u32[]{:S(2)}) collective-permute-start(bf16[1,128,256]{2,1,0:T(8,128)(2,1)S(1)} %get-tuple-element.33), channel_id=1, source_target_pairs={{0,5},{1,4},{2,7},{3,6},{4,1},{5,0},{6,3},{7,2},{8,13},{9,12},{10,... | collective-permute-start | bytes 196616 | tf_op jit(solution)/shard_map/ppermute | solution.py:377
  120.2 6.7 %collective-permute-start.10 = (bf16[1,128,256]{2,1,0:T(8,128)(2,1)S(1)}, bf16[1,128,256]{2,1,0:T(8,128)(2,1)S(1)}, u32[]{:S(2)}, u32[]{:S(2)}) collective-permute-start(bf16[1,128,256]{2,1,0:T(8,128)(2,1)S(1)} %get-tuple-element.34), channel_id=1, source_target_pairs={{0,6},{1,7},{2,4},{3,5},{4,2},{5,3},{6,0},{7,1},{8,14},{9,15},{10,... | collective-permute-start | bytes 196616 | tf_op jit(solution)/shard_map/ppermute | solution.py:377
  122.0 7.1 %collective-permute-start.11 = (bf16[1,128,256]{2,1,0:T(8,128)(2,1)S(1)}, bf16[1,128,256]{2,1,0:T(8,128)(2,1)S(1)}, u32[]{:S(2)}, u32[]{:S(2)}) collective-permute-start(bf16[1,128,256]{2,1,0:T(8,128)(2,1)S(1)} %get-tuple-element.35), channel_id=1, source_target_pairs={{0,7},{1,6},{2,5},{3,4},{4,3},{5,2},{6,1},{7,0},{8,15},{9,14},{10,... | collective-permute-start | bytes 196616 | tf_op jit(solution)/shard_map/ppermute | solution.py:377
  126.8 5.2 %collective-permute-start.8 = (bf16[1,128,256]{2,1,0:T(8,128)(2,1)S(1)}, bf16[1,128,256]{2,1,0:T(8,128)(2,1)S(1)}, u32[]{:S(2)}, u32[]{:S(2)}) collective-permute-start(bf16[1,128,256]{2,1,0:T(8,128)(2,1)S(1)} %get-tuple-element.32.refs_9_), channel_id=1, source_target_pairs={{0,4},{1,5},{2,6},{3,7},{4,0},{5,1},{6,2},{7,3},{8,12},{9,13},{10,... | collective-permute-start | bytes 196616 | tf_op jit(solution)/shard_map/ppermute | solution.py:377
